TPU v7x, 32 devices: a whole 2x2x4 slice. The times are simulated.
32 devices in a mesh: gx: 8 (over z, y), gy: 4 (over x, core).
Axes of the slice: x: 2, y: 2, z: 4, core: 2. Of those that a mesh axis runs over, the one named last changes fastest.
Arguments:
- gas_moisture: float32 [16, 512, 512], P(None, 'gx', 'gy'), may hold values from 0 to 1
- gas_warmth: float32 [16, 512, 512], P(None, 'gx', 'gy'), may hold values from 0.5 to 1.5
- prior_moisture: float32 [16, 512, 512], P(None, 'gx', 'gy'), may hold values from 0 to 1
- prior_warmth: float32 [16, 512, 512], P(None, 'gx', 'gy'), may hold values from 0.5 to 1.5
- flow_speeds: bfloat16 [3, 16, 512, 512], P(None, None, 'gx', 'gy'), may hold values from -4 to 4
- lower_base_cell: int32 [3, 4, 32768], P(None, 'gy', 'gx'), may hold values from 0 to 510, as said below
- trilinear_factors: float32 [8, 4, 32768], P(None, 'gy', 'gx'), may hold values from 0.02 to 0.25
- panel_surface: float32 [4, 32768], P('gy', 'gx'), may hold values from 0.3 to 9
- panel_owner: int32 [4, 32768], P('gy', 'gx'), may hold values from 0 to 159, as said below
- active_panel_tally: int32 [4, 8], P('gy', 'gx'), may hold values from 512 to 4096, as said below
Outputs:
- following_moisture: float32 [16, 512, 512], P(None, 'gx', 'gy')
- following_warmth: float32 [16, 512, 512], P(None, 'gx', 'gy')
Inputs may be any that keep to these rules, and one draw needn't show every extreme that they name: lower_base_cell[0] is a plane of the slab; lower_base_cell[1] lies in the block of 64 cells of the element's gx index, at most 62 past its start; lower_base_cell[2] lies in the block of 128 cells of the element's group, at most 126 past its start. `panel_owner`: every droplet number of a group is named by a live element of that group's row. `active_panel_tally`: every row has a block with exactly 4096 live elements.
All inputs are finite; a program needn't handle non-finite values.
Results may differ from a plain program's by a relative error of at most 0.0003.
Values sent between devices are 32-bit elements; how exact they have to be, the bound alone decides.
No kernel may reach another device: no remote copies, remote signals or barrier semaphores. Data moves between devices by JAX's collectives and lax.ppermute only.
A program may use at most 128 MiB of HBM per device.

v0:
```python
import jax
import jax.numpy as jnp
from jax import lax
from jax.sharding import PartitionSpec as P

DROP_DEV = 20


increment_span = 0.1
diffusivity = 1.0
mass_rate = 2.0
saturation_rate = 2.0
thermal_flux = 1.0
enthalpy_evaporation = 0.5
highest = lax.Precision.HIGHEST


def padded_2(cells, sides, width):
    for axis, dim in sides:
        count = lax.axis_size(axis)
        head = lax.slice_in_dim(cells, 0, width, axis=dim)
        tail = lax.slice_in_dim(cells, cells.shape[dim] - width, cells.shape[dim], axis=dim)
        cells = jnp.concatenate(
            [
                lax.ppermute(tail, axis, [(i, (i + 1) % count) for i in range(count)]),
                cells,
                lax.ppermute(head, axis, [((i + 1) % count, i) for i in range(count)]),
            ],
            axis=dim,
        )
    return cells


def add_direction(total, center, ahead_one, ahead_two, behind_one, behind_two, speed):
    slope = (8.0 * (ahead_one - behind_one) - (ahead_two - behind_two)) / 12.0
    curve = (16.0 * (ahead_one + behind_one) - (ahead_two + behind_two) - 30.0 * center) / 12.0
    return total - speed * slope + diffusivity * curve


def stencil(padded, speed, rows, cols):
    center = padded[:, :, 2 : rows + 2, 2 : cols + 2]
    total = jnp.zeros_like(center)
    total = add_direction(
        total,
        center,
        jnp.roll(center, -1, 1),
        jnp.roll(center, -2, 1),
        jnp.roll(center, 1, 1),
        jnp.roll(center, 2, 1),
        speed[0],
    )
    total = add_direction(
        total,
        center,
        padded[:, :, 3 : rows + 3, 2 : cols + 2],
        padded[:, :, 4 : rows + 4, 2 : cols + 2],
        padded[:, :, 1 : rows + 1, 2 : cols + 2],
        padded[:, :, 0:rows, 2 : cols + 2],
        speed[1],
    )
    total = add_direction(
        total,
        center,
        padded[:, :, 2 : rows + 2, 3 : cols + 3],
        padded[:, :, 2 : rows + 2, 4 : cols + 4],
        padded[:, :, 2 : rows + 2, 1 : cols + 1],
        padded[:, :, 2 : rows + 2, 0:cols],
        speed[2],
    )
    return total


def droplet_table(labels, drops):
    return (labels[:, None] == jnp.arange(drops, dtype=jnp.int32)[None, :]).astype(jnp.float32)


def shards(
    gas_moisture,
    gas_warmth,
    prior_moisture,
    prior_warmth,
    flow_speeds,
    lower_base_cell,
    trilinear_factors,
    panel_surface,
    panel_owner,
    active_panel_tally,
):
    planes, rows, cols = gas_moisture.shape
    plane_rows = planes * rows
    drops = DROP_DEV * lax.axis_size("gx")
    count = panel_surface.shape[1]
    width = min(count, 512)
    blocks = count // width
    living = jnp.arange(count) < active_panel_tally[0, 0]
    plane_base = lower_base_cell[0, 0]
    row_local = lower_base_cell[1, 0] - lax.axis_index("gx") * rows
    col_local = lower_base_cell[2, 0] - lax.axis_index("gy") * cols
    field_rows = jnp.stack([gas_moisture, gas_warmth]).reshape(2 * plane_rows, cols)
    row_ids = jnp.arange(plane_rows, dtype=jnp.int32)[:, None]
    col_ids = jnp.arange(cols, dtype=jnp.int32)[:, None]
    plane_blocks = plane_base.reshape(blocks, width)
    row_blocks = row_local.reshape(blocks, width)
    col_blocks = col_local.reshape(blocks, width)
    weight_blocks = trilinear_factors[:, 0].reshape(8, blocks, width).transpose(1, 0, 2)

    def row_masks(plane_at, row_at):
        masks = {}
        for first in range(2):
            for second in range(2):
                target = (plane_at + first) % planes * rows + row_at + second
                masks[first, second] = (row_ids == target[None, :]).astype(jnp.float32)
        return masks

    def probe(carry, block):
        plane_at, row_at, col_at, weight_at = block
        masks = row_masks(plane_at, row_at)
        value = jnp.zeros((2, width), jnp.float32)
        for third in range(2):
            select = (col_ids == (col_at + third)[None, :]).astype(jnp.float32)
            spread = jnp.dot(field_rows, select, precision=highest).reshape(2, plane_rows, width)
            for first in range(2):
                for second in range(2):
                    picked = jnp.sum(spread * masks[first, second][None], axis=1)
                    value = value + weight_at[first * 4 + second * 2 + third] * picked
        return (carry, value)

    unused, probed = lax.scan(
        probe, jnp.zeros((), jnp.float32), (plane_blocks, row_blocks, col_blocks, weight_blocks)
    )
    probed_values = probed.transpose(1, 0, 2).reshape(2, count)
    moisture_panels = probed_values[0]
    panel_warmth = probed_values[1]
    moist_surface = jnp.where(living, panel_surface[0], jnp.zeros_like(panel_surface[0]))
    particle_labels = panel_owner[0]
    own_table = droplet_table(particle_labels, drops)
    scaled_product = jnp.stack(
        [moist_surface, moist_surface * moisture_panels, moist_surface * panel_warmth], axis=1
    )
    partial_sums = jnp.dot(own_table.T, scaled_product, precision=highest)
    totals = lax.psum(partial_sums, "gx")
    drop_vapour = totals[:, 1] / totals[:, 0]
    particle_warmth = totals[:, 2] / totals[:, 0]
    saturated = 0.5 * jnp.exp(saturation_rate * (particle_warmth - 1.0))
    looked = jnp.dot(
        own_table, jnp.stack([saturated, drop_vapour, particle_warmth], axis=1), precision=highest
    )
    evaporated_amount = (
        mass_rate * moist_surface * (looked[:, 0] - 0.5 * (looked[:, 1] + moisture_panels))
    )
    thermal_energy = (
        moist_surface * thermal_flux * (looked[:, 2] - panel_warmth)
        - enthalpy_evaporation * evaporated_amount
    )
    amount_blocks = (
        jnp.stack([evaporated_amount, thermal_energy]).reshape(2, blocks, width).transpose(1, 0, 2)
    )

    def deposit(total, block):
        plane_at, row_at, col_at, weight_at, amount_at = block
        masks = row_masks(plane_at, row_at)
        for third in range(2):
            select = (col_ids == (col_at + third)[None, :]).astype(jnp.float32)
            spread = jnp.zeros((2, plane_rows, width), jnp.float32)
            for first in range(2):
                for second in range(2):
                    scaled = weight_at[first * 4 + second * 2 + third] * amount_at
                    spread = spread + masks[first, second][None] * scaled[:, None, :]
            total = total + jnp.dot(
                spread.reshape(2 * plane_rows, width), select.T, precision=highest
            )
        return (total, None)

    sources, unused_out = lax.scan(
        deposit,
        jnp.zeros((2 * plane_rows, cols), jnp.float32),
        (plane_blocks, row_blocks, col_blocks, weight_blocks, amount_blocks),
    )
    sources = sources.reshape(2, planes, rows, cols)
    speed = flow_speeds.astype(jnp.float32)
    current_state = jnp.stack([gas_moisture, gas_warmth])
    epoch_history = jnp.stack([gas_moisture, gas_warmth, prior_moisture, prior_warmth])
    padded = padded_2(epoch_history, (("gx", 2), ("gy", 3)), 2)
    total = stencil(padded, speed, rows, cols)
    change = 1.5 * total[:2] - 0.5 * total[2:]
    stepped = current_state + increment_span * change + sources
    return (stepped[0], stepped[1])


def solution(mesh):
    return jax.shard_map(
        shards,
        mesh=mesh,
        in_specs=(
            P(None, "gx", "gy"),
            P(None, "gx", "gy"),
            P(None, "gx", "gy"),
            P(None, "gx", "gy"),
            P(None, None, "gx", "gy"),
            P(None, "gy", "gx"),
            P(None, "gy", "gx"),
            P("gy", "gx"),
            P("gy", "gx"),
            P("gy", "gx"),
        ),
        out_specs=(P(None, "gx", "gy"), P(None, "gx", "gy")),
        check_vma=False,
    )
```

profile of v0, /device:TPU:0, one launch (start us, length us, event | category | flops | bytes accessed | tf_op | source)
XLA Modules:
  0.0 614.5 jit_solution(3248415624938876126)
XLA Ops:
  3.1 6.0 collective-permute-start
  17.1 428.1 %while.28 = (s32[]{:T(128)}, f32[8,2,512]{1,2,0:T(8,128)}, f32[8,8,512]{2,1,0:T(8,128)S(1)}, s32[8,512]{1,0:T(8,128)}, f32[2048,128]{1,0:T(8,128)S(1)}, /*index=...) while((s32[]{:T(128)}, f32[8,2,512]{1,2,0:T(8,128)}, ...), condition=%wide.region_9.10_spmd.clone.clone, body=%wide.region_0.9_spmd.clone.clone.sunk | while | flops 3242481664 | bytes 79808896 | solution.py:128
  21.7 6.6 %reshape.1089 = f32[2,1024,512]{1,0,2:T(2,128)} reshape(f32[2048,512]{0,1:T(8,128)} %convolution_bitcast_fusion.4) | data formatting | bytes 8388608 | tf_op jit(solution)/shard_map/while/body/eval_jaxpr/reshape | solution.py:121
  30.0 5.1 convolution_bitcast_fusion.5
  35.1 6.6 %reshape.1090 = f32[2,1024,512]{1,0,2:T(2,128)} reshape(f32[2048,512]{0,1:T(8,128)} %convolution_bitcast_fusion.5) | data formatting | bytes 8388608 | tf_op jit(solution)/shard_map/while/body/eval_jaxpr/reshape | solution.py:121
  45.1 22.7 %multiply_reduce_fusion.9 = (f32[2,512]{0,1:T(8,128)S(1)}, f32[2,512]{0,1:T(8,128)}, f32[2,512]{0,1:T(8,128)}, f32[2,512]{0,1:T(8,128)}, f32[2,512]{0,1:T(8,128)...) fusion(f32[2,1024,512]{1,0,2:T(2,128)S(1)} %copy-done.1, f32[1024,512]{0,1:T(8,128)S(1)} %fusion.107, ...), kind=kLoop, calls=%fused_computation.11.clone.1 | loop fusion | flops 16769024 | bytes 16809984 | tf_op jit(solution)/shard_map/while/body/eval_jaxpr/reduce_sum | solution.py:124
  75.2 6.6 %reshape.1089 = f32[2,1024,512]{1,0,2:T(2,128)} reshape(f32[2048,512]{0,1:T(8,128)} %convolution_bitcast_fusion.4) | data formatting | bytes 8388608 | tf_op jit(solution)/shard_map/while/body/eval_jaxpr/reshape | solution.py:121
  83.5 5.1 convolution_bitcast_fusion.5
  88.6 6.6 %reshape.1090 = f32[2,1024,512]{1,0,2:T(2,128)} reshape(f32[2048,512]{0,1:T(8,128)} %convolution_bitcast_fusion.5) | data formatting | bytes 8388608 | tf_op jit(solution)/shard_map/while/body/eval_jaxpr/reshape | solution.py:121
  98.6 22.7 %multiply_reduce_fusion.9 = (f32[2,512]{0,1:T(8,128)S(1)}, f32[2,512]{0,1:T(8,128)}, f32[2,512]{0,1:T(8,128)}, f32[2,512]{0,1:T(8,128)}, f32[2,512]{0,1:T(8,128)...) fusion(f32[2,1024,512]{1,0,2:T(2,128)S(1)} %copy-done.1, f32[1024,512]{0,1:T(8,128)S(1)} %fusion.107, ...), kind=kLoop, calls=%fused_computation.11.clone.1 | loop fusion | flops 16769024 | bytes 16809984 | tf_op jit(solution)/shard_map/while/body/eval_jaxpr/reduce_sum | solution.py:124
  128.7 6.6 %reshape.1089 = f32[2,1024,512]{1,0,2:T(2,128)} reshape(f32[2048,512]{0,1:T(8,128)} %convolution_bitcast_fusion.4) | data formatting | bytes 8388608 | tf_op jit(solution)/shard_map/while/body/eval_jaxpr/reshape | solution.py:121
  137.0 5.1 convolution_bitcast_fusion.5
  142.1 6.6 %reshape.1090 = f32[2,1024,512]{1,0,2:T(2,128)} reshape(f32[2048,512]{0,1:T(8,128)} %convolution_bitcast_fusion.5) | data formatting | bytes 8388608 | tf_op jit(solution)/shard_map/while/body/eval_jaxpr/reshape | solution.py:121
  152.1 22.7 %multiply_reduce_fusion.9 = (f32[2,512]{0,1:T(8,128)S(1)}, f32[2,512]{0,1:T(8,128)}, f32[2,512]{0,1:T(8,128)}, f32[2,512]{0,1:T(8,128)}, f32[2,512]{0,1:T(8,128)...) fusion(f32[2,1024,512]{1,0,2:T(2,128)S(1)} %copy-done.1, f32[1024,512]{0,1:T(8,128)S(1)} %fusion.107, ...), kind=kLoop, calls=%fused_computation.11.clone.1 | loop fusion | flops 16769024 | bytes 16809984 | tf_op jit(solution)/shard_map/while/body/eval_jaxpr/reduce_sum | solution.py:124
  182.2 6.6 %reshape.1089 = f32[2,1024,512]{1,0,2:T(2,128)} reshape(f32[2048,512]{0,1:T(8,128)} %convolution_bitcast_fusion.4) | data formatting | bytes 8388608 | tf_op jit(solution)/shard_map/while/body/eval_jaxpr/reshape | solution.py:121
  190.5 5.1 convolution_bitcast_fusion.5
  195.6 6.6 %reshape.1090 = f32[2,1024,512]{1,0,2:T(2,128)} reshape(f32[2048,512]{0,1:T(8,128)} %convolution_bitcast_fusion.5) | data formatting | bytes 8388608 | tf_op jit(solution)/shard_map/while/body/eval_jaxpr/reshape | solution.py:121
  205.6 22.7 %multiply_reduce_fusion.9 = (f32[2,512]{0,1:T(8,128)S(1)}, f32[2,512]{0,1:T(8,128)}, f32[2,512]{0,1:T(8,128)}, f32[2,512]{0,1:T(8,128)}, f32[2,512]{0,1:T(8,128)...) fusion(f32[2,1024,512]{1,0,2:T(2,128)S(1)} %copy-done.1, f32[1024,512]{0,1:T(8,128)S(1)} %fusion.107, ...), kind=kLoop, calls=%fused_computation.11.clone.1 | loop fusion | flops 16769024 | bytes 16809984 | tf_op jit(solution)/shard_map/while/body/eval_jaxpr/reduce_sum | solution.py:124
  235.7 6.6 %reshape.1089 = f32[2,1024,512]{1,0,2:T(2,128)} reshape(f32[2048,512]{0,1:T(8,128)} %convolution_bitcast_fusion.4) | data formatting | bytes 8388608 | tf_op jit(solution)/shard_map/while/body/eval_jaxpr/reshape | solution.py:121
  244.0 5.1 convolution_bitcast_fusion.5
  249.1 6.6 %reshape.1090 = f32[2,1024,512]{1,0,2:T(2,128)} reshape(f32[2048,512]{0,1:T(8,128)} %convolution_bitcast_fusion.5) | data formatting | bytes 8388608 | tf_op jit(solution)/shard_map/while/body/eval_jaxpr/reshape | solution.py:121
  259.1 22.7 %multiply_reduce_fusion.9 = (f32[2,512]{0,1:T(8,128)S(1)}, f32[2,512]{0,1:T(8,128)}, f32[2,512]{0,1:T(8,128)}, f32[2,512]{0,1:T(8,128)}, f32[2,512]{0,1:T(8,128)...) fusion(f32[2,1024,512]{1,0,2:T(2,128)S(1)} %copy-done.1, f32[1024,512]{0,1:T(8,128)S(1)} %fusion.107, ...), kind=kLoop, calls=%fused_computation.11.clone.1 | loop fusion | flops 16769024 | bytes 16809984 | tf_op jit(solution)/shard_map/while/body/eval_jaxpr/reduce_sum | solution.py:124
  289.3 6.6 %reshape.1089 = f32[2,1024,512]{1,0,2:T(2,128)} reshape(f32[2048,512]{0,1:T(8,128)} %convolution_bitcast_fusion.4) | data formatting | bytes 8388608 | tf_op jit(solution)/shard_map/while/body/eval_jaxpr/reshape | solution.py:121
  297.6 5.1 convolution_bitcast_fusion.5
  302.6 6.6 %reshape.1090 = f32[2,1024,512]{1,0,2:T(2,128)} reshape(f32[2048,512]{0,1:T(8,128)} %convolution_bitcast_fusion.5) | data formatting | bytes 8388608 | tf_op jit(solution)/shard_map/while/body/eval_jaxpr/reshape | solution.py:121
  312.7 22.7 %multiply_reduce_fusion.9 = (f32[2,512]{0,1:T(8,128)S(1)}, f32[2,512]{0,1:T(8,128)}, f32[2,512]{0,1:T(8,128)}, f32[2,512]{0,1:T(8,128)}, f32[2,512]{0,1:T(8,128)...) fusion(f32[2,1024,512]{1,0,2:T(2,128)S(1)} %copy-done.1, f32[1024,512]{0,1:T(8,128)S(1)} %fusion.107, ...), kind=kLoop, calls=%fused_computation.11.clone.1 | loop fusion | flops 16769024 | bytes 16809984 | tf_op jit(solution)/shard_map/while/body/eval_jaxpr/reduce_sum | solution.py:124
  342.8 6.6 %reshape.1089 = f32[2,1024,512]{1,0,2:T(2,128)} reshape(f32[2048,512]{0,1:T(8,128)} %convolution_bitcast_fusion.4) | data formatting | bytes 8388608 | tf_op jit(solution)/shard_map/while/body/eval_jaxpr/reshape | solution.py:121
  351.1 5.1 convolution_bitcast_fusion.5
  356.2 6.6 %reshape.1090 = f32[2,1024,512]{1,0,2:T(2,128)} reshape(f32[2048,512]{0,1:T(8,128)} %convolution_bitcast_fusion.5) | data formatting | bytes 8388608 | tf_op jit(solution)/shard_map/while/body/eval_jaxpr/reshape | solution.py:121
  366.2 22.7 %multiply_reduce_fusion.9 = (f32[2,512]{0,1:T(8,128)S(1)}, f32[2,512]{0,1:T(8,128)}, f32[2,512]{0,1:T(8,128)}, f32[2,512]{0,1:T(8,128)}, f32[2,512]{0,1:T(8,128)...) fusion(f32[2,1024,512]{1,0,2:T(2,128)S(1)} %copy-done.1, f32[1024,512]{0,1:T(8,128)S(1)} %fusion.107, ...), kind=kLoop, calls=%fused_computation.11.clone.1 | loop fusion | flops 16769024 | bytes 16809984 | tf_op jit(solution)/shard_map/while/body/eval_jaxpr/reduce_sum | solution.py:124
  396.3 6.6 %reshape.1089 = f32[2,1024,512]{1,0,2:T(2,128)} reshape(f32[2048,512]{0,1:T(8,128)} %convolution_bitcast_fusion.4) | data formatting | bytes 8388608 | tf_op jit(solution)/shard_map/while/body/eval_jaxpr/reshape | solution.py:121
  404.6 5.1 convolution_bitcast_fusion.5
  409.7 6.6 %reshape.1090 = f32[2,1024,512]{1,0,2:T(2,128)} reshape(f32[2048,512]{0,1:T(8,128)} %convolution_bitcast_fusion.5) | data formatting | bytes 8388608 | tf_op jit(solution)/shard_map/while/body/eval_jaxpr/reshape | solution.py:121
  419.7 22.7 %multiply_reduce_fusion.9 = (f32[2,512]{0,1:T(8,128)S(1)}, f32[2,512]{0,1:T(8,128)}, f32[2,512]{0,1:T(8,128)}, f32[2,512]{0,1:T(8,128)}, f32[2,512]{0,1:T(8,128)...) fusion(f32[2,1024,512]{1,0,2:T(2,128)S(1)} %copy-done.1, f32[1024,512]{0,1:T(8,128)S(1)} %fusion.107, ...), kind=kLoop, calls=%fused_computation.11.clone.1 | loop fusion | flops 16769024 | bytes 16809984 | tf_op jit(solution)/shard_map/while/body/eval_jaxpr/reduce_sum | solution.py:124
  451.4 22.0 %psum.7 = f32[160,3]{0,1:T(4,128)S(1)} all-reduce(f32[160,3]{0,1:T(4,128)S(1)} %fusion.45), channel_id=1, replica_groups=mesh['gx'=8,'gy'=4] {'gx'}, use_global_device_ids=true, to_apply=%region_10.11 | all-reduce | flops 480 | bytes 3840 | tf_op jit(solution)/shard_map/psum | solution.py:141
  474.5 102.7 %while.29 = (s32[]{:T(128)}, f32[2048,128]{1,0:T(8,128)S(1)}, s32[8,512]{1,0:T(8,128)S(1)}, s32[8,512]{1,0:T(8,128)S(1)}, f32[8,8,512]{2,1,0:T(8,128)S(1)}, /*in...) while((s32[]{:T(128)}, f32[2048,128]{1,0:T(8,128)S(1)}, ...), condition=%wide.region_12.13_spmd.clone.clone, body=%wide.region_11.12_spmd.clone.clone.sunk | while | flops 3241040896 | bytes 54675772 | solution.py:174
  476.6 4.3 multiply_add_fusion.4
  480.9 4.4 convolution_add_fusion.4
  489.4 4.3 multiply_add_fusion.4
  493.7 4.4 convolution_add_fusion.4
  502.2 4.3 multiply_add_fusion.4
  506.6 4.4 convolution_add_fusion.4
  519.4 4.4 convolution_add_fusion.4
  532.2 4.4 convolution_add_fusion.4
  545.1 4.4 convolution_add_fusion.4
  557.9 4.4 convolution_add_fusion.4
  570.7 4.4 convolution_add_fusion.4
  600.5 12.5 %multiply_add_fusion.2 = f32[4,16,64,128]{3,2,1,0:T(8,128)S(1)} fusion(f32[4,16,68,2]{3,2,1,0:T(8,128)} %copy.34, f32[4,16,2,128]{3,2,1,0:T(2,128)} %collective-permute-done, f32[1,16,64,128]{3,2,1,0:T(8,128)S(1)} %bitcast.282, f32[1,16,64,128]{3,2,1,0:T(8,128)S(1)} %bitcast.286, f32[1,16,64,128]{3,2,1,0:T(8,128)S(1)} %bitcast.270, ...), kind=kLoop, calls=%fused_computation.148 | loop fusion | flops 37224448 | bytes 22745088 | tf_op jit(solution)/shard_map/add | solution.py:37
  (265 shorter events, 196.1 us)
Async XLA Ops:
  2.3 11.2 %copy-start.4 = (f32[4,16,64,128]{3,2,1,0:T(8,128)}, f32[4,16,64,128]{3,2,1,0:T(8,128)S(1)}, u32[]{:S(2)}) copy-start(f32[4,16,64,128]{3,2,1,0:T(8,128)S(1)} %pad_maximum_fusion.16) | copy-start | bytes 6291460
  3.1 577.2 %collective-permute-start = (f32[4,16,2,128]{3,2,1,0:T(2,128)}, f32[4,16,2,128]{3,2,1,0:T(2,128)}, u32[]{:S(2)}, u32[]{:S(2)}) collective-permute-start(f32[4,16,2,128]{3,2,1,0:T(2,128)} %get-tuple-element.527), channel_id=1, source_target_pairs={{4,0},{8,4},{12,8},{16,12},{20,16},{24,20},{28,24},{0,28},{5,1},{9... | collective-permute-start | bytes 196616 | tf_op jit(solution)/shard_map/ppermute | solution.py:27
  9.1 571.2 %collective-permute-start.1 = (f32[4,16,2,128]{3,2,1,0:T(2,128)}, f32[4,16,2,128]{3,2,1,0:T(2,128)}, u32[]{:S(2)}, u32[]{:S(2)}) collective-permute-start(f32[4,16,2,128]{3,2,1,0:T(2,128)} %get-tuple-element.526), channel_id=1, source_target_pairs={{0,4},{4,8},{8,12},{12,16},{16,20},{20,24},{24,28},{28,0},{1,5},{5... | collective-permute-start | bytes 196616 | tf_op jit(solution)/shard_map/ppermute | solution.py:25
  13.5 2.4 copy-start.14
  13.5 2.6 copy-start.12
  17.1 4.5 copy-start.2
  41.6 3.4 copy-start.1
  67.8 2.8 copy-start.3
  70.6 4.5 copy-start.2
  95.1 3.4 copy-start.1
  121.3 2.9 copy-start.3
  124.1 4.5 copy-start.2
  148.7 3.4 copy-start.1
  174.8 2.9 copy-start.3
  177.7 4.5 copy-start.2
  202.2 3.4 copy-start.1
  228.3 2.9 copy-start.3
  231.2 4.5 copy-start.2
  255.7 3.4 copy-start.1
  281.8 2.9 copy-start.3
  284.7 4.5 copy-start.2
  309.2 3.4 copy-start.1
  335.4 2.9 copy-start.3
  338.2 4.5 copy-start.2
  362.7 3.4 copy-start.1
  388.9 2.9 copy-start.3
  391.7 4.5 copy-start.2
  416.3 3.4 copy-start.1
  442.4 2.9 copy-start.3
  445.3 4.8 copy-start.13
  445.3 4.8 copy-start.15
  445.3 29.2 %copy-start.5 = (f32[2048,128]{1,0:T(8,128)S(1)}, f32[2048,128]{1,0:T(8,128)}, u32[]{:S(2)}) copy-start(f32[2048,128]{1,0:T(8,128)} %custom-call) | copy-start | bytes 3145732
  474.5 102.7 %copy-start.11 = (bf16[3,16,64,128]{3,2,1,0:T(8,128)(2,1)S(1)}, bf16[3,16,64,128]{3,2,1,0:T(8,128)(2,1)}, u32[]{:S(2)}) copy-start(bf16[3,16,64,128]{3,2,1,0:T(8,128)(2,1)} %param.18) | copy-start | bytes 2359300
  480.9 4.4 copy-start
  493.7 4.4 copy-start
  506.6 4.4 copy-start
  519.4 4.4 copy-start
  532.2 4.4 copy-start
  545.1 4.4 copy-start
  557.9 4.4 copy-start
  570.7 4.4 copy-start
  577.4 2.9 copy-start.6
  577.4 2.9 copy-start.7
  577.4 2.9 copy-start.8
  577.4 2.9 copy-start.9
  587.5 6.7 %collective-permute-start.2 = (f32[4,16,68,2]{2,1,3,0:T(8,128)}, f32[4,16,68,2]{2,1,3,0:T(8,128)}, u32[]{:S(2)}, u32[]{:S(2)}) collective-permute-start(f32[4,16,68,2]{2,1,3,0:T(8,128)} %copy.33), channel_id=1, source_target_pairs={{1,0},{2,1},{3,2},{0,3},{5,4},{6,5},{7,6},{4,7},{9,8},{10,9},{11,1... | collective-permute-start | bytes 104456 | tf_op jit(solution)/shard_map/ppermute | solution.py:27
  590.6 6.8 %collective-permute-start.3 = (f32[4,16,68,2]{2,1,3,0:T(8,128)}, f32[4,16,68,2]{2,1,3,0:T(8,128)}, u32[]{:S(2)}, u32[]{:S(2)}) collective-permute-start(f32[4,16,68,2]{2,1,3,0:T(8,128)} %copy.35), channel_id=1, source_target_pairs={{0,1},{1,2},{2,3},{3,0},{4,5},{5,6},{6,7},{7,4},{8,9},{9,10},{10,1... | collective-permute-start | bytes 104456 | tf_op jit(solution)/shard_map/ppermute | solution.py:25
  594.2 6.3 %copy-start.10 = (f32[4,2,64,128]{3,2,1,0:T(8,128)S(1)}, f32[4,2,64,128]{3,2,1,0:T(8,128)}, u32[]{:S(2)}) copy-start(f32[4,2,64,128]{3,2,1,0:T(8,128)} %get-tuple-element.522) | copy-start | bytes 786436
where the time goes:
time: 619 us; the launch traced here: 615 us
  other arithmetic  321 us (52%)
  local copies, waits for them, and re-layouts  138 us (22%)
  matrix products  125 us (20%)
  blocking collectives  22 us (4%)
  starting transfers between devices  6.52 us (1%)
    reduce_sum x8, other arithmetic, probe(): picked = jnp.sum(spread * masks[first, second][None], axis=1)  182 us
    reshape x16, local copies, waits for them, and re-layouts, probe(): jnp.dot(field_rows, select, precision=highest).reshape(2, plane_rows, width)  105 us
    dot_general x16, matrix products, probe(): jnp.dot(field_rows, select, precision=highest).reshape(2, plane_rows, width)  70.9 us
    dot_general x16, matrix products, deposit(): jnp.dot(spread.reshape(2 * plane_rows, width), select.T, precision=highest)  51.8 us
    convert_element_type x64, other arithmetic, row_masks(): masks[first, second] = (row_ids == target[None, :]).astype(jnp.float32)  47.8 us
    add x8, other arithmetic, deposit(): spread = spread + masks[first, second][None] * scaled[:, None, :]  34.6 us
    dynamic_update_slice x8, other arithmetic, shards(): lax.scan(probe, jnp.zeros((), jnp.float32), (plane_blocks, row_blocks, co...  22.7 us
    psum x1, blocking collectives, shards(): totals = lax.psum(partial_sums, 'gx')  22 us
  transfers between devices with their start and end apart: 4, of which 0 were waited for; matrix products, arithmetic and copies ran while one was open for 90% of the time, Pallas kernels for 0%

commit v1 on v0

v1 whole, which is shorter than its diff:
```python
import functools

import jax
import jax.numpy as jnp
from jax import lax
from jax.experimental import pallas as pl
from jax.experimental.pallas import tpu as pltpu
from jax.sharding import PartitionSpec as P

DROP_DEV = 20
LANES = 128
HALF = 64

increment_span = 0.1
diffusivity = 1.0
mass_rate = 2.0
saturation_rate = 2.0
thermal_flux = 1.0
enthalpy_evaporation = 0.5

VMEM = pl.BlockSpec(memory_space=pltpu.VMEM)
SMEM = pl.BlockSpec(memory_space=pltpu.SMEM)
COPIES = 4


def iota(shape, dim):
    return lax.broadcasted_iota(jnp.int32, shape, dim)


def pick(values, index):
    return jnp.take_along_axis(values, index, axis=1, mode="promise_in_bounds")


def swap_rows(x, even):
    return jnp.where(even, pltpu.roll(x, 7, 0), pltpu.roll(x, 1, 0))


def edges_kernel(moist, warm, old_moist, old_warm, blend, top, bottom, left, right):
    planes, rows, cols = moist.shape
    for field, (now, old) in enumerate(((moist, old_moist), (warm, old_warm))):
        for pair in range(planes // 2):
            halves = []
            for plane in (2 * pair, 2 * pair + 1):
                mixed = 1.5 * now[plane] - 0.5 * old[plane]
                blend[field, plane] = mixed
                top[field, plane] = mixed[0:2]
                bottom[field, plane] = mixed[rows - 2 : rows]
                halves.append(mixed)
            turned = jnp.concatenate(halves, axis=0).T
            at = (field * planes // 2 + pair) * 2 * rows
            left[:, pl.ds(at, 2 * rows)] = turned[0:2]
            right[:, pl.ds(at, 2 * rows)] = turned[cols - 2 : cols]


def gather_kernel(index, tally, moist, warm, factors, surface, owner, scaled, fronts, sums, table, terms):
    planes, rows, cols = moist.shape
    groups = surface.shape[0]
    drops = sums.shape[1]
    for plane in range(planes):
        below = (plane - 1) % planes
        table[pl.ds(plane * rows * 4, rows, stride=4), :] = moist[plane]
        table[pl.ds(plane * rows * 4 + 1, rows, stride=4), :] = warm[plane]
        table[pl.ds(below * rows * 4 + 2, rows, stride=4), :] = moist[plane]
        table[pl.ds(below * rows * 4 + 3, rows, stride=4), :] = warm[plane]
    live = tally[0, 0]

    def group_step(group, carry):
        lane = iota((8, LANES), 1)
        sub = iota((8, LANES), 0)
        even = (sub & 1) == 0
        even_lane = (lane & 1) == 0
        raw = factors[pl.ds(group, 8, stride=groups), :]
        raw = jnp.where(
            (sub == 2) | (sub == 3),
            pltpu.roll(raw, 6, 0),
            jnp.where((sub == 4) | (sub == 5), pltpu.roll(raw, 2, 0), raw),
        )
        area = jnp.broadcast_to(surface[pl.ds(group, 1), :], (8, LANES))
        area = jnp.where(lane + group * LANES < live, area, 0.0)
        values = []
        for half in range(2):
            found = jnp.zeros((8, LANES), jnp.float32)
            for j in range(HALF):
                word = index[group * LANES + half * HALF + j]
                row = lax.shift_right_logical(word, 7)
                entry = table[pl.ds(row * 4, 8), :]
                entry = pltpu.roll(entry, word & 127, 1)
                found = jnp.where(lane >= 2 * j, entry, found)
            spread = (lane >> 1) + half * HALF
            weight = pick(raw, spread)
            weight = jnp.where((lane & 1) == (sub & 1), weight, swap_rows(weight, even))
            value = found * weight
            value = value + pltpu.roll(value, 2, 0)
            value = value + pltpu.roll(value, 4, 0)
            value = value + jnp.where(even_lane, pltpu.roll(value, 127, 1), pltpu.roll(value, 1, 1))
            at = pl.ds((group * 2 + half) * 8, 8)
            scaled[at, :] = weight * pick(area, spread)
            fronts[at, :] = jnp.where(even, value, value - 0.5 * swap_rows(value, even))
            values.append(pick(value, (lane * 2) & 127))
        value = jnp.where(lane < HALF, values[0], values[1])
        term = jnp.where(sub == 2, 1.0, value) * area
        high = term.astype(jnp.bfloat16).astype(jnp.float32)
        both = jnp.concatenate([high, term - high], axis=0).astype(jnp.bfloat16)
        terms[:, pl.ds(pl.multiple_of(group * LANES, LANES), LANES)] = both
        return carry

    lax.fori_loop(0, groups, group_step, 0)
    total = jnp.zeros((16, drops), jnp.float32)
    span = 8
    for first in range(0, groups, span):
        tables = []
        for group in range(first, first + span):
            label = jnp.broadcast_to(owner[pl.ds(group, 1), :], (drops, LANES))
            tables.append((label == iota((drops, LANES), 0)).astype(jnp.float32).astype(jnp.bfloat16))
        total = total + lax.dot_general(
            terms[:, first * LANES : (first + span) * LANES],
            jnp.concatenate(tables, axis=1),
            (((1,), (1,)), ((), ())),
            preferred_element_type=jnp.float32,
        )
    sums[...] = total[0:8] + total[8:16]


def stencil_kernel(blend, moist, warm, speed, above, below, left, right, out_moist, out_warm, padded, side):
    planes, rows, cols = moist.shape
    for field in range(2):
        for plane in range(planes):
            padded[field, plane, 8 : rows + 8, :] = blend[field, plane]
            padded[field, plane, 6:8, :] = above[field, plane]
            padded[field, plane, rows + 8 : rows + 10, :] = below[field, plane]
        for pair in range(planes // 2):
            slot = field * (planes // 2) + pair
            at = slot * 2 * rows
            block = jnp.concatenate(
                [
                    right[:, pl.ds(at, 2 * rows)],
                    jnp.zeros((cols - 4, 2 * rows), jnp.float32),
                    left[:, pl.ds(at, 2 * rows)],
                ],
                axis=0,
            )
            side[pl.ds(slot * 2 * rows, 2 * rows), :] = block.T
    lane = iota((rows, cols), 1)
    fraction = increment_span / 12.0

    def plane_step(plane, carry):
        speeds = [speed[k, plane].astype(jnp.float32) * fraction for k in range(3)]
        for field, (now, out) in enumerate(((moist, out_moist), (warm, out_warm))):
            center = padded[field, plane, 8 : rows + 8, :]
            edge = side[pl.ds(pl.multiple_of((field * planes + plane) * rows, rows), rows), :]
            wrap = lambda shift: padded[field, lax.rem(plane + shift + planes, planes), 8 : rows + 8, :]
            shift = lambda by: padded[field, plane, 8 + by : rows + 8 + by, :]
            around = [
                (wrap(1), wrap(2), wrap(-1), wrap(-2)),
                (shift(1), shift(2), shift(-1), shift(-2)),
                (
                    pltpu.roll(jnp.where(lane < 1, edge, center), cols - 1, 1),
                    pltpu.roll(jnp.where(lane < 2, edge, center), cols - 2, 1),
                    pltpu.roll(jnp.where(lane >= cols - 1, edge, center), 1, 1),
                    pltpu.roll(jnp.where(lane >= cols - 2, edge, center), 2, 1),
                ),
            ]
            near = 0.0
            far = 0.0
            total = now[plane] - (90.0 * diffusivity * fraction) * center
            for k, (ahead_one, ahead_two, behind_one, behind_two) in enumerate(around):
                near = near + (ahead_one + behind_one)
                far = far + (ahead_two + behind_two)
                total = total - speeds[k] * (8.0 * (ahead_one - behind_one) - (ahead_two - behind_two))
            out[plane] = total + (diffusivity * fraction) * (16.0 * near - far)
        return carry

    lax.fori_loop(0, planes, plane_step, 0)


def scatter_kernel(index, scaled, fronts, owner, sums, start_moist, start_warm, out_moist, out_warm, *banks):
    planes, rows, cols = start_moist.shape
    groups = owner.shape[0]
    drops = sums.shape[1]
    size = banks[0].shape[0]

    def clear(step, carry):
        for bank in banks:
            bank[pl.ds(pl.multiple_of(step * 128, 128), 128), :] = jnp.zeros((128, cols), jnp.float32)
        return carry

    lax.fori_loop(0, size // 128, clear, 0)
    totals = sums[...]
    drop_vapour = totals[0:1] / totals[2:3]
    drop_warmth = totals[1:2] / totals[2:3]
    saturated = 0.5 * jnp.exp(saturation_rate * (drop_warmth - 1.0))
    for_mass = 2.0 * saturated - drop_vapour
    for_heat = drop_warmth - 0.5 * for_mass
    wide = (8, drops)
    both = jnp.where(
        (iota(wide, 0) & 1) == 0, jnp.broadcast_to(for_mass, wide), jnp.broadcast_to(for_heat, wide)
    )
    pieces = []
    for at in range(0, drops, LANES):
        piece = both[:, at : min(at + LANES, drops)]
        if piece.shape[1] < LANES:
            piece = jnp.concatenate([piece, jnp.zeros((8, LANES - piece.shape[1]), jnp.float32)], axis=1)
        pieces.append(piece)

    def group_step(group, carry):
        lane = iota((8, LANES), 1)
        label = jnp.broadcast_to(owner[pl.ds(group, 1), :], (8, LANES))
        looked = pick(pieces[0], label & 127)
        for number in range(1, len(pieces)):
            looked = jnp.where(label >= number * LANES, pick(pieces[number], label & 127), looked)
        for half in range(2):
            at = pl.ds((group * 2 + half) * 8, 8)
            value = scaled[at, :] * (pick(looked, (lane >> 1) + half * HALF) - fronts[at, :])
            for j in range(HALF):
                word = index[group * LANES + half * HALF + j]
                row = lax.shift_right_logical(word, 7)
                entry = jnp.where((lane >> 1) == j, value, 0.0)
                entry = pltpu.roll(entry, (128 - word) & 127, 1)
                banks[j % len(banks)][pl.ds(row * 4, 8), :] += entry
        return carry

    lax.fori_loop(0, groups, group_step, 0)
    for plane in range(planes):
        before = (plane - 1) % planes
        for field, (start, out) in enumerate(((start_moist, out_moist), (start_warm, out_warm))):
            total = start[plane]
            for bank in banks:
                total = total + bank[pl.ds(plane * rows * 4 + field, rows, stride=4), :]
                total = total + bank[pl.ds(before * rows * 4 + 2 + field, rows, stride=4), :]
            out[plane] = total


def params(megabytes=40):
    return pltpu.CompilerParams(vmem_limit_bytes=megabytes << 20)


def shards(
    gas_moisture,
    gas_warmth,
    prior_moisture,
    prior_warmth,
    flow_speeds,
    lower_base_cell,
    trilinear_factors,
    panel_surface,
    panel_owner,
    active_panel_tally,
):
    planes, rows, cols = gas_moisture.shape
    drops = DROP_DEV * lax.axis_size("gx")
    count = panel_surface.shape[1]
    groups = count // LANES
    f32 = jnp.float32
    shape = jax.ShapeDtypeStruct
    row_local = lower_base_cell[1, 0] - lax.axis_index("gx") * rows
    col_local = lower_base_cell[2, 0] - lax.axis_index("gy") * cols
    turn = (2 * (jnp.arange(count, dtype=jnp.int32) % HALF) - col_local) & 127
    index = (lower_base_cell[0, 0] * rows + row_local) * 128 + turn
    factors = trilinear_factors.reshape(8 * groups, LANES)
    surface = panel_surface.reshape(groups, LANES)
    owner = panel_owner.reshape(groups, LANES)
    field = shape((planes, rows, cols), f32)

    blend, top, bottom, left, right = pl.pallas_call(
        edges_kernel,
        out_shape=(
            shape((2, planes, rows, cols), f32),
            shape((2, planes, 2, cols), f32),
            shape((2, planes, 2, cols), f32),
            shape((2, 2 * planes * rows), f32),
            shape((2, 2 * planes * rows), f32),
        ),
        in_specs=[VMEM] * 4,
        out_specs=[VMEM] * 5,
        compiler_params=params(),
        name="edges",
    )(gas_moisture, gas_warmth, prior_moisture, prior_warmth)

    def around(axis, head, tail):
        size = lax.axis_size(axis)
        onward = [(i, (i + 1) % size) for i in range(size)]
        backward = [((i + 1) % size, i) for i in range(size)]
        return lax.ppermute(tail, axis, onward), lax.ppermute(head, axis, backward)

    above, below = around("gx", top, bottom)
    from_left, from_right = around("gy", left, right)

    scaled, fronts, sums = pl.pallas_call(
        gather_kernel,
        out_shape=(
            shape((2 * groups * 8, LANES), f32),
            shape((2 * groups * 8, LANES), f32),
            shape((8, drops), f32),
        ),
        in_specs=[SMEM, SMEM] + [VMEM] * 5,
        out_specs=[VMEM] * 3,
        scratch_shapes=[
            pltpu.VMEM((planes * rows * 4 + 8, cols), f32),
            pltpu.VMEM((16, count), jnp.bfloat16),
        ],
        compiler_params=params(),
        name="gather",
    )(index, active_panel_tally, gas_moisture, gas_warmth, factors, surface, owner)

    totals = lax.psum(sums, "gx")

    start_moist, start_warm = pl.pallas_call(
        stencil_kernel,
        out_shape=(field, field),
        in_specs=[VMEM] * 8,
        out_specs=[VMEM] * 2,
        scratch_shapes=[
            pltpu.VMEM((2, planes, rows + 16, cols), f32),
            pltpu.VMEM((2 * planes * rows, cols), f32),
        ],
        compiler_params=params(),
        name="stencil",
    )(blend, gas_moisture, gas_warmth, flow_speeds, above, below, from_left, from_right)

    size = planes * rows * 4 + 128
    return pl.pallas_call(
        scatter_kernel,
        out_shape=(field, field),
        in_specs=[SMEM] + [VMEM] * 6,
        out_specs=[VMEM] * 2,
        scratch_shapes=[pltpu.VMEM((size, cols), f32)] * COPIES,
        compiler_params=params(),
        name="scatter",
    )(index, scaled, fronts, owner, totals, start_moist, start_warm)


def solution(mesh):
    return jax.shard_map(
        shards,
        mesh=mesh,
        in_specs=(
            P(None, "gx", "gy"),
            P(None, "gx", "gy"),
            P(None, "gx", "gy"),
            P(None, "gx", "gy"),
            P(None, None, "gx", "gy"),
            P(None, "gy", "gx"),
            P(None, "gy", "gx"),
            P("gy", "gx"),
            P("gy", "gx"),
            P("gy", "gx"),
        ),
        out_specs=(P(None, "gx", "gy"), P(None, "gx", "gy")),
        check_vma=False,
    )
```

time: 619 us -> 72.3 us (0.12)
  other arithmetic: 321 us -> 0.05 us
  local copies, waits for them, and re-layouts: 138 us -> 6.21 us
  matrix products: 125 us -> 0 us
  Pallas kernels: 0 us -> 36.8 us
    reduce_sum x8 -> x0, other arithmetic: 182 us -> none  [probe(): picked = jnp.sum(spread * masks[first, second][None], axis=1)]
    dot_general x34 -> x0, matrix products: 125 us -> none  [the longest x16 70.9 us: probe(): jnp.dot(field_rows, select, precision=highest).reshape(2, plane_rows, width)]
    reshape x16 -> x0, local copies, waits for them, and re-layouts: 105 us -> none  [probe(): jnp.dot(field_rows, select, precision=highest).reshape(2, plane_rows, width)]
    add x26 -> x1, other arithmetic: 59.6 us -> 0.01 us  [shards(): index = (lower_base_cell[0, 0] * rows + row_local) * 128 + turn]
    convert_element_type x65 -> x0, other arithmetic: 48 us -> none  [the longest x64 47.8 us: row_masks(): masks[first, second] = (row_ids == target[None, :]).astype(jnp.float32)]
    pallas_call x0 -> x4, Pallas kernels: none -> 36.8 us  [the longest x1 17.2 us: shards(): pl.pallas_call(scatter_kernel, out_shape=(field, field), in_specs=[SMEM]...]
    dynamic_update_slice x8 -> x0, other arithmetic: 22.7 us -> none  [shards(): lax.scan(probe, jnp.zeros((), jnp.float32), (plane_blocks, row_blocks, co...]
    slice x25 -> x0, local copies, waits for them, and re-layouts: 21.4 us -> none  [the longest x3 6.73 us: padded_2(): lax.slice_in_dim(cells, cells.shape[dim] - width, cells.shape[dim], axis=...]
  transfers between devices with their start and end apart: 4 -> 4, of which waited for: 0 -> 0; matrix products, arithmetic and copies ran while one was open for 90% -> 0% of each run, Pallas kernels for 0% -> 21%
where the time goes in v1:
time: 72.3 us; the launch traced here: 71.7 us
  Pallas kernels  36.8 us (51%)
  blocking collectives  19.5 us (27%)
  starting transfers between devices  7.75 us (11%)
  local copies, waits for them, and re-layouts  6.21 us (9%)
  between operations  1.43 us (2%)
    psum x1, blocking collectives, shards(): totals = lax.psum(sums, 'gx')  19.5 us
    pallas_call x1, Pallas kernels, shards(): pl.pallas_call(scatter_kernel, out_shape=(field, field), in_specs=[SMEM]...  17.2 us
    pallas_call x1, Pallas kernels, shards(): pl.pallas_call(gather_kernel, out_shape=(shape((2 * groups * 8, LANES), f...  15 us
    unnamed x26, local copies, waits for them, and re-layouts  6.21 us
    ppermute x2, starting transfers between devices, around(): lax.ppermute(head, axis, backward)  4.78 us
    pallas_call x1, Pallas kernels, shards(): pl.pallas_call(stencil_kernel, out_shape=(field, field), in_specs=[VMEM]...  3.62 us
    ppermute x2, starting transfers between devices, around(): lax.ppermute(tail, axis, onward)  2.97 us
  transfers between devices with their start and end apart: 4, of which 0 were waited for; matrix products, arithmetic and copies ran while one was open for 0% of the time, Pallas kernels for 21%

profile of v1, /device:TPU:0, one launch (start us, length us, event | category | flops | bytes accessed | tf_op | source)
XLA Modules:
  0.0 71.7 jit_solution(2927779120953410308)
XLA Ops:
  0.6 0.0 copy-start
  0.6 1.0 %copy-done = f32[16,64,128]{2,1,0:T(8,128)S(1)} copy-done((f32[16,64,128]{2,1,0:T(8,128)S(1)}, f32[16,64,128]{2,1,0:T(8,128)}, u32[]{:S(2)}) %copy-start) | copy-done | bytes 524312
  1.7 0.0 copy-start.2
  1.7 1.0 %copy-done.2 = f32[16,64,128]{2,1,0:T(8,128)S(1)} copy-done((f32[16,64,128]{2,1,0:T(8,128)S(1)}, f32[16,64,128]{2,1,0:T(8,128)}, u32[]{:S(2)}) %copy-start.2) | copy-done | bytes 524312
  2.7 0.0 copy-start.5
  2.7 1.0 %copy-done.5 = f32[16,64,128]{2,1,0:T(8,128)S(1)} copy-done((f32[16,64,128]{2,1,0:T(8,128)S(1)}, f32[16,64,128]{2,1,0:T(8,128)}, u32[]{:S(2)}) %copy-start.5) | copy-done | bytes 524312
  3.8 0.0 copy-start.6
  3.8 1.0 %copy-done.6 = f32[16,64,128]{2,1,0:T(8,128)S(1)} copy-done((f32[16,64,128]{2,1,0:T(8,128)S(1)}, f32[16,64,128]{2,1,0:T(8,128)}, u32[]{:S(2)}) %copy-start.6) | copy-done | bytes 524312
  4.8 0.0 copy-start.12
  4.8 0.0 copy-start.1
  4.8 0.0 copy-start.3
  4.8 0.0 copy-start.7
  4.8 1.0 %edges.1 = (f32[2,16,64,128]{3,2,1,0:T(8,128)S(1)}, f32[2,16,2,128]{3,2,1,0:T(2,128)}, f32[2,16,2,128]{3,2,1,0:T(2,128)}, f32[2,2048]{1,0:T(2,128)}, f32[2,2048]{1,0:T(2,128)}) custom-call(f32[16,64,128]{2,1,0:T(8,128)S(1)} %copy-done, f32[16,64,128]{2,1,0:T(8,128)S(1)} %copy-done.2, f32[16,64,128]{2,1,0:T(8,128)S(1)} %copy-done.5, f32[16,64,128]{2,1,0:T(8,128)S(1)} %copy-done.6), custom_call_target="tpu_custom_call" | custom-call | tf_op jit(solution)/shard_map/edges/pallas_call | solution.py:264
  5.8 0.0 copy-start.4
  5.8 3.0 %collective-permute-start = (f32[2,16,2,128]{3,2,1,0:T(2,128)}, f32[2,16,2,128]{3,2,1,0:T(2,128)}, u32[]{:S(2)}, u32[]{:S(2)}) collective-permute-start(f32[2,16,2,128]{3,2,1,0:T(2,128)} %get-tuple-element.16), channel_id=1, source_target_pairs={{0,4},{4,8},{8,12},{12,16},{16,20},{20,24},{24,28},{28,0},{1,5},{5... | collective-permute-start | bytes 98312 | tf_op jit(solution)/shard_map/ppermute | solution.py:283
  8.7 3.0 %collective-permute-start.1 = (f32[2,16,2,128]{3,2,1,0:T(2,128)}, f32[2,16,2,128]{3,2,1,0:T(2,128)}, u32[]{:S(2)}, u32[]{:S(2)}) collective-permute-start(f32[2,16,2,128]{3,2,1,0:T(2,128)} %get-tuple-element.17), channel_id=1, source_target_pairs={{4,0},{8,4},{12,8},{16,12},{20,16},{24,20},{28,24},{0,28},{5,1},{9... | collective-permute-start | bytes 98312 | tf_op jit(solution)/shard_map/ppermute | solution.py:283
  11.8 0.0 collective-permute-start.2
  11.8 1.7 %collective-permute-start.3 = (f32[2,2048]{1,0:T(2,128)}, f32[2,2048]{1,0:T(2,128)}, u32[]{:S(2)}, u32[]{:S(2)}) collective-permute-start(f32[2,2048]{1,0:T(2,128)} %get-tuple-element.19), channel_id=1, source_target_pairs={{1,0},{2,1},{3,2},{0,3},{5,4},{6,5},{7,6},{4,7},{9,8},{10,9},{11,1... | collective-permute-start | bytes 49160 | tf_op jit(solution)/shard_map/ppermute | solution.py:283
  13.5 0.0 copy-done.12
  14.2 0.0 copy-done.1
  14.2 0.0 copy-done.3
  14.3 0.0 copy-done.7
  14.3 0.0 copy-start.8
  14.3 0.7 copy-done.8
  15.0 0.0 copy-start.10
  15.0 0.7 copy-done.10
  15.7 15.0 %gather.1 = (f32[512,128]{1,0:T(8,128)S(1)}, f32[512,128]{1,0:T(8,128)S(1)}, f32[8,160]{1,0:T(8,128)S(1)}) custom-call(s32[4096]{0:T(1024)S(1)} %fusion.3.index, s32[1,1]{1,0:T(1,128)S(6)} %copy.12.tally, f32[16,64,128]{2,1,0:T(8,128)S(1)} %copy-done.1, f32[16,64,128]{2,1,0:T(8,128)S(1)} %copy-done.3, f32[256,128]{1,0:T(8,128)S(1)} %bitcast.5, ...), custom_call_target="tpu_custom_call" | custom-call | tf_op jit(solution)/shard_map/gather/pallas_call | solution.py:288
  30.7 0.0 copy-start.11
  30.7 0.6 copy-done.11
  31.3 19.5 %psum.7.sums = f32[8,160]{1,0:T(8,128)S(1)} all-reduce(f32[8,160]{1,0:T(8,128)} %copy-done.11), channel_id=1, replica_groups=mesh['gx'=8,'gy'=4] {'gx'}, use_global_device_ids=true, to_apply=%region_0.1 | all-reduce | flops 1280 | bytes 10240 | tf_op jit(solution)/shard_map/psum | solution.py:305
  50.8 0.0 collective-permute-done.2.left
  50.8 0.0 collective-permute-done.3.right
  50.8 0.0 collective-permute-done.above
  50.8 0.0 collective-permute-done.1.below
  50.8 0.0 copy-done.4
  50.8 0.0 copy-start.9
  50.9 3.6 %stencil.1 = (f32[16,64,128]{2,1,0:T(8,128)S(1)}, f32[16,64,128]{2,1,0:T(8,128)S(1)}) custom-call(f32[2,16,64,128]{3,2,1,0:T(8,128)S(1)} %get-tuple-element.15.blend, f32[16,64,128]{2,1,0:T(8,128)S(1)} %copy-done.1, f32[16,64,128]{2,1,0:T(8,128)S(1)} %copy-done.3, bf16[3,16,64,128]{3,2,1,0:T(8,128)(2,1)S(1)} %copy-done.4, ...), custom_call_target="tpu_custom_call" | custom-call | tf_op jit(solution)/shard_map/stencil/pallas_call | solution.py:307
  54.5 0.0 copy-done.9
  54.5 17.2 %scatter.1 = (f32[16,64,128]{2,1,0:T(8,128)}, f32[16,64,128]{2,1,0:T(8,128)}) custom-call(s32[4096]{0:T(1024)S(1)} %fusion.3.index, f32[512,128]{1,0:T(8,128)S(1)} %get-tuple-element.12.scaled, f32[512,128]{1,0:T(8,128)S(1)} %get-tuple-element.13.fronts, s32[32,128]{1,0:T(8,128)S(1)} %bitcast.7, f32[8,160]{1,0:T(8,128)S(1)} %psum.7.sums, ...), custom_call_target="tpu_custom_call" | custom-call | tf_op jit(solution)/shard_map/scatter/pallas_call | solution.py:321
  (2 shorter events, 0.0 us)
Async XLA Ops:
  0.6 1.0 %copy-start = (f32[16,64,128]{2,1,0:T(8,128)S(1)}, f32[16,64,128]{2,1,0:T(8,128)}, u32[]{:S(2)}) copy-start(f32[16,64,128]{2,1,0:T(8,128)} %moist.5) | copy-start | bytes 1572868
  1.7 1.0 %copy-start.2 = (f32[16,64,128]{2,1,0:T(8,128)S(1)}, f32[16,64,128]{2,1,0:T(8,128)}, u32[]{:S(2)}) copy-start(f32[16,64,128]{2,1,0:T(8,128)} %warm.5) | copy-start | bytes 1572868
  2.7 1.0 %copy-start.5 = (f32[16,64,128]{2,1,0:T(8,128)S(1)}, f32[16,64,128]{2,1,0:T(8,128)}, u32[]{:S(2)}) copy-start(f32[16,64,128]{2,1,0:T(8,128)} %old_moist.1) | copy-start | bytes 1572868
  3.8 1.0 %copy-start.6 = (f32[16,64,128]{2,1,0:T(8,128)S(1)}, f32[16,64,128]{2,1,0:T(8,128)}, u32[]{:S(2)}) copy-start(f32[16,64,128]{2,1,0:T(8,128)} %old_warm.1) | copy-start | bytes 1572868
  4.8 8.7 %copy-start.12 = (s32[3,1,4096]{2,1,0:T(1,128)S(1)}, s32[3,1,4096]{2,1,0:T(1,128)}, u32[]{:S(2)}) copy-start(s32[3,1,4096]{2,1,0:T(1,128)} %param.15) | copy-start | bytes 147460
  4.8 9.4 %copy-start.1 = (f32[16,64,128]{2,1,0:T(8,128)S(1)}, f32[16,64,128]{2,1,0:T(8,128)}, u32[]{:S(2)}) copy-start(f32[16,64,128]{2,1,0:T(8,128)} %moist.5) | copy-start | bytes 1572868
  4.8 9.4 %copy-start.3 = (f32[16,64,128]{2,1,0:T(8,128)S(1)}, f32[16,64,128]{2,1,0:T(8,128)}, u32[]{:S(2)}) copy-start(f32[16,64,128]{2,1,0:T(8,128)} %warm.5) | copy-start | bytes 1572868
  4.8 9.4 %copy-start.7 = (f32[8,1,4096]{2,1,0:T(1,128)S(1)}, f32[8,1,4096]{2,1,0:T(1,128)}, u32[]{:S(2)}) copy-start(f32[8,1,4096]{2,1,0:T(1,128)} %param.16) | copy-start | bytes 393220
  5.8 45.1 %copy-start.4 = (bf16[3,16,64,128]{3,2,1,0:T(8,128)(2,1)S(1)}, bf16[3,16,64,128]{3,2,1,0:T(8,128)(2,1)}, u32[]{:S(2)}) copy-start(bf16[3,16,64,128]{3,2,1,0:T(8,128)(2,1)} %speed.1) | copy-start | bytes 2359300
  5.8 45.0 %collective-permute-start = (f32[2,16,2,128]{3,2,1,0:T(2,128)}, f32[2,16,2,128]{3,2,1,0:T(2,128)}, u32[]{:S(2)}, u32[]{:S(2)}) collective-permute-start(f32[2,16,2,128]{3,2,1,0:T(2,128)} %get-tuple-element.16), channel_id=1, source_target_pairs={{0,4},{4,8},{8,12},{12,16},{16,20},{20,24},{24,28},{28,0},{1,5},{5... | collective-permute-start | bytes 98312 | tf_op jit(solution)/shard_map/ppermute | solution.py:283
  8.7 42.1 %collective-permute-start.1 = (f32[2,16,2,128]{3,2,1,0:T(2,128)}, f32[2,16,2,128]{3,2,1,0:T(2,128)}, u32[]{:S(2)}, u32[]{:S(2)}) collective-permute-start(f32[2,16,2,128]{3,2,1,0:T(2,128)} %get-tuple-element.17), channel_id=1, source_target_pairs={{4,0},{8,4},{12,8},{16,12},{20,16},{24,20},{28,24},{0,28},{5,1},{9... | collective-permute-start | bytes 98312 | tf_op jit(solution)/shard_map/ppermute | solution.py:283
  11.8 39.0 %collective-permute-start.2 = (f32[2,2048]{1,0:T(2,128)}, f32[2,2048]{1,0:T(2,128)}, u32[]{:S(2)}, u32[]{:S(2)}) collective-permute-start(f32[2,2048]{1,0:T(2,128)} %get-tuple-element.18), channel_id=1, source_target_pairs={{0,1},{1,2},{2,3},{3,0},{4,5},{5,6},{6,7},{7,4},{8,9},{9,10},{10,1... | collective-permute-start | bytes 49160 | tf_op jit(solution)/shard_map/ppermute | solution.py:283
  11.8 39.0 %collective-permute-start.3 = (f32[2,2048]{1,0:T(2,128)}, f32[2,2048]{1,0:T(2,128)}, u32[]{:S(2)}, u32[]{:S(2)}) collective-permute-start(f32[2,2048]{1,0:T(2,128)} %get-tuple-element.19), channel_id=1, source_target_pairs={{1,0},{2,1},{3,2},{0,3},{5,4},{6,5},{7,6},{4,7},{9,8},{10,9},{11,1... | collective-permute-start | bytes 49160 | tf_op jit(solution)/shard_map/ppermute | solution.py:283
  14.3 0.7 %copy-start.8 = (s32[1,4096]{1,0:T(1,128)S(1)}, s32[1,4096]{1,0:T(1,128)}, u32[]{:S(2)}) copy-start(s32[1,4096]{1,0:T(1,128)} %param.18) | copy-start | bytes 49156
  15.0 0.7 %copy-start.10 = (f32[1,4096]{1,0:T(1,128)S(1)}, f32[1,4096]{1,0:T(1,128)}, u32[]{:S(2)}) copy-start(f32[1,4096]{1,0:T(1,128)} %param.17) | copy-start | bytes 49156
  30.7 0.6 copy-start.11
  50.8 3.6 %copy-start.9 = (s32[1,4096]{1,0:T(1,128)S(1)}, s32[1,4096]{1,0:T(1,128)}, u32[]{:S(2)}) copy-start(s32[1,4096]{1,0:T(1,128)} %param.18) | copy-start | bytes 49156

commit v2 on v1

--- a/solution.py
+++ b/solution.py
@@ -19,8 +19,10 @@
 enthalpy_evaporation = 0.5
 
 VMEM = pl.BlockSpec(memory_space=pltpu.VMEM)
+HBM = pl.BlockSpec(memory_space=pltpu.HBM)
 SMEM = pl.BlockSpec(memory_space=pltpu.SMEM)
 COPIES = 4
+UNROLL = 4
 
 
 def iota(shape, dim):
@@ -35,13 +37,31 @@
     return jnp.where(even, pltpu.roll(x, 7, 0), pltpu.roll(x, 1, 0))
 
 
-def edges_kernel(moist, warm, old_moist, old_warm, blend, top, bottom, left, right):
+def edges_kernel(moist, warm, old_moist, old_warm, blend, top, bottom, left, right, stage, arrived):
     planes, rows, cols = moist.shape
+    parts = 2
+    step = planes // parts
+    copies = []
     for field, (now, old) in enumerate(((moist, old_moist), (warm, old_warm))):
-        for pair in range(planes // 2):
+        for part in range(parts):
+            span = pl.ds(part * step, step)
+            row = []
+            for level, source in enumerate((now, old)):
+                slot = (field * parts + part) * 2 + level
+                row.append(
+                    pltpu.make_async_copy(
+                        source.at[span], stage.at[2 * field + level, span], arrived.at[slot]
+                    )
+                )
+                row[-1].start()
+            copies.append((field, part, row))
+    for field, part, row in copies:
+        for copy in row:
+            copy.wait()
+        for pair in range(part * step // 2, (part + 1) * step // 2):
             halves = []
             for plane in (2 * pair, 2 * pair + 1):
-                mixed = 1.5 * now[plane] - 0.5 * old[plane]
+                mixed = 1.5 * stage[2 * field, plane] - 0.5 * stage[2 * field + 1, plane]
                 blend[field, plane] = mixed
                 top[field, plane] = mixed[0:2]
                 bottom[field, plane] = mixed[rows - 2 : rows]
@@ -52,7 +72,7 @@
             right[:, pl.ds(at, 2 * rows)] = turned[cols - 2 : cols]
 
 
-def gather_kernel(index, tally, moist, warm, factors, surface, owner, scaled, fronts, sums, table, terms):
+def gather_kernel(start, turn, tally, moist, warm, factors, surface, owner, scaled, fronts, sums, table):
     planes, rows, cols = moist.shape
     groups = surface.shape[0]
     drops = sums.shape[1]
@@ -63,61 +83,70 @@
         table[pl.ds(below * rows * 4 + 2, rows, stride=4), :] = moist[plane]
         table[pl.ds(below * rows * 4 + 3, rows, stride=4), :] = warm[plane]
     live = tally[0, 0]
-
-    def group_step(group, carry):
-        lane = iota((8, LANES), 1)
-        sub = iota((8, LANES), 0)
-        even = (sub & 1) == 0
-        even_lane = (lane & 1) == 0
-        raw = factors[pl.ds(group, 8, stride=groups), :]
-        raw = jnp.where(
-            (sub == 2) | (sub == 3),
-            pltpu.roll(raw, 6, 0),
-            jnp.where((sub == 4) | (sub == 5), pltpu.roll(raw, 2, 0), raw),
-        )
-        area = jnp.broadcast_to(surface[pl.ds(group, 1), :], (8, LANES))
-        area = jnp.where(lane + group * LANES < live, area, 0.0)
-        values = []
-        for half in range(2):
+    lane = iota((8, LANES), 1)
+    sub = iota((8, LANES), 0)
+    even = (sub & 1) == 0
+    even_lane = (lane & 1) == 0
+
+    def raw(block):
+        blocks = []
+        for half in range(2 * UNROLL):
             found = jnp.zeros((8, LANES), jnp.float32)
             for j in range(HALF):
-                word = index[group * LANES + half * HALF + j]
-                row = lax.shift_right_logical(word, 7)
-                entry = table[pl.ds(row * 4, 8), :]
-                entry = pltpu.roll(entry, word & 127, 1)
+                at = block * (UNROLL * LANES) + half * HALF + j
+                entry = pltpu.roll(table[pl.ds(start[at], 8), :], turn[at], 1)
                 found = jnp.where(lane >= 2 * j, entry, found)
-            spread = (lane >> 1) + half * HALF
-            weight = pick(raw, spread)
-            weight = jnp.where((lane & 1) == (sub & 1), weight, swap_rows(weight, even))
-            value = found * weight
-            value = value + pltpu.roll(value, 2, 0)
-            value = value + pltpu.roll(value, 4, 0)
-            value = value + jnp.where(even_lane, pltpu.roll(value, 127, 1), pltpu.roll(value, 1, 1))
-            at = pl.ds((group * 2 + half) * 8, 8)
-            scaled[at, :] = weight * pick(area, spread)
-            fronts[at, :] = jnp.where(even, value, value - 0.5 * swap_rows(value, even))
-            values.append(pick(value, (lane * 2) & 127))
-        value = jnp.where(lane < HALF, values[0], values[1])
-        term = jnp.where(sub == 2, 1.0, value) * area
-        high = term.astype(jnp.bfloat16).astype(jnp.float32)
-        both = jnp.concatenate([high, term - high], axis=0).astype(jnp.bfloat16)
-        terms[:, pl.ds(pl.multiple_of(group * LANES, LANES), LANES)] = both
-        return carry
-
-    lax.fori_loop(0, groups, group_step, 0)
-    total = jnp.zeros((16, drops), jnp.float32)
-    span = 8
-    for first in range(0, groups, span):
+            blocks.append(found)
+        return blocks
+
+    def refine(block, blocks, total):
+        terms = []
         tables = []
-        for group in range(first, first + span):
+        for unit in range(UNROLL):
+            group = block * UNROLL + unit
+            corner = factors[pl.ds(group, 8, stride=groups), :]
+            corner = jnp.where(
+                (sub == 2) | (sub == 3),
+                pltpu.roll(corner, 6, 0),
+                jnp.where((sub == 4) | (sub == 5), pltpu.roll(corner, 2, 0), corner),
+            )
+            other = swap_rows(corner, even)
+            area = jnp.broadcast_to(surface[pl.ds(group, 1), :], (8, LANES))
+            area = jnp.where(lane + group * LANES < live, area, 0.0)
+            values = []
+            for half in range(2):
+                spread = (lane >> 1) + half * HALF
+                weight = jnp.where(even_lane == even, pick(corner, spread), pick(other, spread))
+                value = blocks[2 * unit + half] * weight
+                value = value + pltpu.roll(value, 2, 0)
+                value = value + pltpu.roll(value, 4, 0)
+                value = value + jnp.where(even_lane, pltpu.roll(value, 127, 1), pltpu.roll(value, 1, 1))
+                at = pl.ds(pl.multiple_of((group * 2 + half) * 8, 8), 8)
+                scaled[at, :] = weight * pick(area, spread)
+                fronts[at, :] = jnp.where(even, value, value - 0.5 * pltpu.roll(value, 1, 0))
+                values.append(pick(value, (lane * 2) & 127))
+            value = jnp.where(lane < HALF, values[0], values[1])
+            term = jnp.where(sub == 2, 1.0, value) * area
+            high = term.astype(jnp.bfloat16).astype(jnp.float32)
+            terms.append(jnp.concatenate([high, term - high], axis=0).astype(jnp.bfloat16))
             label = jnp.broadcast_to(owner[pl.ds(group, 1), :], (drops, LANES))
             tables.append((label == iota((drops, LANES), 0)).astype(jnp.float32).astype(jnp.bfloat16))
-        total = total + lax.dot_general(
-            terms[:, first * LANES : (first + span) * LANES],
+        return total + lax.dot_general(
+            jnp.concatenate(terms, axis=1),
             jnp.concatenate(tables, axis=1),
             (((1,), (1,)), ((), ())),
             preferred_element_type=jnp.float32,
         )
+
+    def step(block, carry):
+        total, *blocks = carry
+        later = raw(block)
+        return (refine(block - 1, blocks, total), *later)
+
+    count = groups // UNROLL
+    carry = (jnp.zeros((16, drops), jnp.float32), *raw(0))
+    total, *blocks = lax.fori_loop(1, count, step, carry)
+    total = refine(count - 1, blocks, total)
     sums[...] = total[0:8] + total[8:16]
 
 
@@ -173,7 +202,7 @@
     lax.fori_loop(0, planes, plane_step, 0)
 
 
-def scatter_kernel(index, scaled, fronts, owner, sums, start_moist, start_warm, out_moist, out_warm, *banks):
+def scatter_kernel(begin, turn, scaled, fronts, owner, sums, start_moist, start_warm, out_moist, out_warm, *banks):
     planes, rows, cols = start_moist.shape
     groups = owner.shape[0]
     drops = sums.shape[1]
@@ -202,24 +231,36 @@
             piece = jnp.concatenate([piece, jnp.zeros((8, LANES - piece.shape[1]), jnp.float32)], axis=1)
         pieces.append(piece)
 
-    def group_step(group, carry):
-        lane = iota((8, LANES), 1)
-        label = jnp.broadcast_to(owner[pl.ds(group, 1), :], (8, LANES))
-        looked = pick(pieces[0], label & 127)
-        for number in range(1, len(pieces)):
-            looked = jnp.where(label >= number * LANES, pick(pieces[number], label & 127), looked)
-        for half in range(2):
-            at = pl.ds((group * 2 + half) * 8, 8)
-            value = scaled[at, :] * (pick(looked, (lane >> 1) + half * HALF) - fronts[at, :])
+    lane = iota((8, LANES), 1)
+
+    def ready(block):
+        values = []
+        for unit in range(UNROLL):
+            group = block * UNROLL + unit
+            label = jnp.broadcast_to(owner[pl.ds(group, 1), :], (8, LANES))
+            looked = pick(pieces[0], label & 127)
+            for number in range(1, len(pieces)):
+                looked = jnp.where(label >= number * LANES, pick(pieces[number], label & 127), looked)
+            for half in range(2):
+                at = pl.ds(pl.multiple_of((group * 2 + half) * 8, 8), 8)
+                values.append(scaled[at, :] * (pick(looked, (lane >> 1) + half * HALF) - fronts[at, :]))
+        return values
+
+    def spill(block, values):
+        for half in range(2 * UNROLL):
             for j in range(HALF):
-                word = index[group * LANES + half * HALF + j]
-                row = lax.shift_right_logical(word, 7)
-                entry = jnp.where((lane >> 1) == j, value, 0.0)
-                entry = pltpu.roll(entry, (128 - word) & 127, 1)
-                banks[j % len(banks)][pl.ds(row * 4, 8), :] += entry
-        return carry
-
-    lax.fori_loop(0, groups, group_step, 0)
+                at = block * (UNROLL * LANES) + half * HALF + j
+                entry = jnp.where((lane >> 1) == j, values[half], 0.0)
+                banks[j % len(banks)][pl.ds(begin[at], 8), :] += pltpu.roll(entry, turn[at], 1)
+
+    def step(block, values):
+        later = ready(block + 1)
+        spill(block, values)
+        return tuple(later)
+
+    count = groups // UNROLL
+    values = lax.fori_loop(0, count - 1, step, tuple(ready(0)))
+    spill(count - 1, values)
     for plane in range(planes):
         before = (plane - 1) % planes
         for field, (start, out) in enumerate(((start_moist, out_moist), (start_warm, out_warm))):
@@ -255,7 +296,8 @@
     row_local = lower_base_cell[1, 0] - lax.axis_index("gx") * rows
     col_local = lower_base_cell[2, 0] - lax.axis_index("gy") * cols
     turn = (2 * (jnp.arange(count, dtype=jnp.int32) % HALF) - col_local) & 127
-    index = (lower_base_cell[0, 0] * rows + row_local) * 128 + turn
+    back = (128 - turn) & 127
+    start = (lower_base_cell[0, 0] * rows + row_local) * 4
     factors = trilinear_factors.reshape(8 * groups, LANES)
     surface = panel_surface.reshape(groups, LANES)
     owner = panel_owner.reshape(groups, LANES)
@@ -270,8 +312,9 @@
             shape((2, 2 * planes * rows), f32),
             shape((2, 2 * planes * rows), f32),
         ),
-        in_specs=[VMEM] * 4,
+        in_specs=[HBM] * 4,
         out_specs=[VMEM] * 5,
+        scratch_shapes=[pltpu.VMEM((4, planes, rows, cols), f32), pltpu.SemaphoreType.DMA((8,))],
         compiler_params=params(),
         name="edges",
     )(gas_moisture, gas_warmth, prior_moisture, prior_warmth)
@@ -292,17 +335,21 @@
             shape((2 * groups * 8, LANES), f32),
             shape((8, drops), f32),
         ),
-        in_specs=[SMEM, SMEM] + [VMEM] * 5,
+        in_specs=[SMEM] * 3 + [VMEM] * 5,
         out_specs=[VMEM] * 3,
-        scratch_shapes=[
-            pltpu.VMEM((planes * rows * 4 + 8, cols), f32),
-            pltpu.VMEM((16, count), jnp.bfloat16),
-        ],
+        scratch_shapes=[pltpu.VMEM((planes * rows * 4 + 8, cols), f32)],
         compiler_params=params(),
         name="gather",
-    )(index, active_panel_tally, gas_moisture, gas_warmth, factors, surface, owner)
-
-    totals = lax.psum(sums, "gx")
+    )(start, turn, active_panel_tally, gas_moisture, gas_warmth, factors, surface, owner)
+
+    totals = sums
+    size = lax.axis_size("gx")
+    if size & (size - 1):
+        totals = lax.psum(totals, "gx")
+    else:
+        for bit in range(size.bit_length() - 1):
+            swap = [(i, i ^ (1 << bit)) for i in range(size)]
+            totals = totals + lax.ppermute(totals, "gx", swap)
 
     start_moist, start_warm = pl.pallas_call(
         stencil_kernel,
@@ -321,12 +368,12 @@
     return pl.pallas_call(
         scatter_kernel,
         out_shape=(field, field),
-        in_specs=[SMEM] + [VMEM] * 6,
+        in_specs=[SMEM] * 2 + [VMEM] * 6,
         out_specs=[VMEM] * 2,
         scratch_shapes=[pltpu.VMEM((size, cols), f32)] * COPIES,
         compiler_params=params(),
         name="scatter",
-    )(index, scaled, fronts, owner, totals, start_moist, start_warm)
+    )(start, back, scaled, fronts, owner, totals, start_moist, start_warm)
 
 
 def solution(mesh):

time: 72.3 us -> 48.3 us (0.67)
  blocking collectives: 19.5 us -> 0 us
  Pallas kernels: 36.8 us -> 22.6 us
  waiting for transfers between devices: 0.01 us -> 10.9 us
  local copies, waits for them, and re-layouts: 6.21 us -> 4.19 us
  starting transfers between devices: 7.75 us -> 8.81 us
    psum x1 -> x0, blocking collectives: 19.5 us -> none  [shards(): totals = lax.psum(sums, 'gx')]
    ppermute x0 -> x3, waiting for transfers between devices: none -> 10.9 us  [shards(): totals = totals + lax.ppermute(totals, 'gx', swap)]
    pallas_call x1, Pallas kernels: 17.2 us -> 10.3 us  [shards(): pl.pallas_call(scatter_kernel, out_shape=(field, field), in_specs=[SMEM]...]
    pallas_call x1, Pallas kernels: 15 us -> 8.77 us  [shards(): pl.pallas_call(gather_kernel, out_shape=(shape((2 * groups * 8, LANES), f...]
    unnamed x26 -> x22, local copies, waits for them, and re-layouts: 6.21 us -> 4.19 us
    ppermute x0 -> x3, starting transfers between devices: none -> 1.01 us  [shards(): totals = totals + lax.ppermute(totals, 'gx', swap)]
    pallas_call x1, Pallas kernels: 3.62 us -> 2.76 us  [shards(): pl.pallas_call(stencil_kernel, out_shape=(field, field), in_specs=[VMEM]...]
  transfers between devices with their start and end apart: 4 -> 7, of which waited for: 0 -> 3; matrix products, arithmetic and copies ran while one was open for 0% -> 0% of each run, Pallas kernels for 21% -> 18%
where the time goes in v2:
time: 48.3 us; the launch traced here: 48 us
  Pallas kernels  22.6 us (47%)
  waiting for transfers between devices  10.9 us (23%)
  starting transfers between devices  8.81 us (18%)
  local copies, waits for them, and re-layouts  4.19 us (9%)
  between operations  1.43 us (3%)
    ppermute x3, waiting for transfers between devices, shards(): totals = totals + lax.ppermute(totals, 'gx', swap)  10.9 us
    pallas_call x1, Pallas kernels, shards(): pl.pallas_call(scatter_kernel, out_shape=(field, field), in_specs=[SMEM]...  10.3 us
    pallas_call x1, Pallas kernels, shards(): pl.pallas_call(gather_kernel, out_shape=(shape((2 * groups * 8, LANES), f...  8.77 us
    ppermute x2, starting transfers between devices, around(): lax.ppermute(head, axis, backward)  5.03 us
    unnamed x22, local copies, waits for them, and re-layouts  4.19 us
    ppermute x2, starting transfers between devices, around(): lax.ppermute(tail, axis, onward)  2.77 us
    pallas_call x1, Pallas kernels, shards(): pl.pallas_call(stencil_kernel, out_shape=(field, field), in_specs=[VMEM]...  2.76 us
    ppermute x3, starting transfers between devices, shards(): totals = totals + lax.ppermute(totals, 'gx', swap)  1.01 us
  transfers between devices with their start and end apart: 7, of which 3 were waited for; matrix products, arithmetic and copies ran while one was open for 0% of the time, Pallas kernels for 18%

profile of v2, /device:TPU:0, one launch (start us, length us, event | category | flops | bytes accessed | tf_op | source)
XLA Modules:
  0.0 48.0 jit_solution(9878787994913785833)
XLA Ops:
  0.6 0.0 copy-start
  0.6 1.0 %copy-done = f32[16,64,128]{2,1,0:T(8,128)S(1)} copy-done((f32[16,64,128]{2,1,0:T(8,128)S(1)}, f32[16,64,128]{2,1,0:T(8,128)}, u32[]{:S(2)}) %copy-start) | copy-done | bytes 524312
  1.7 0.0 copy-start.2
  1.7 1.0 %copy-done.2 = f32[16,64,128]{2,1,0:T(8,128)S(1)} copy-done((f32[16,64,128]{2,1,0:T(8,128)S(1)}, f32[16,64,128]{2,1,0:T(8,128)}, u32[]{:S(2)}) %copy-start.2) | copy-done | bytes 524312
  2.7 0.0 copy-start.5
  2.7 1.0 %copy-done.5 = f32[16,64,128]{2,1,0:T(8,128)S(1)} copy-done((f32[16,64,128]{2,1,0:T(8,128)S(1)}, f32[16,64,128]{2,1,0:T(8,128)}, u32[]{:S(2)}) %copy-start.5) | copy-done | bytes 524312
  3.8 0.0 copy-start.6
  3.8 1.0 %copy-done.6 = f32[16,64,128]{2,1,0:T(8,128)S(1)} copy-done((f32[16,64,128]{2,1,0:T(8,128)S(1)}, f32[16,64,128]{2,1,0:T(8,128)}, u32[]{:S(2)}) %copy-start.6) | copy-done | bytes 524312
  4.8 0.0 copy-start.10
  4.8 0.0 copy-start.1
  4.8 0.0 copy-start.3
  4.8 0.0 copy-start.7
  4.8 0.0 copy-start.8
  4.8 0.0 copy-start.9
  4.8 0.8 %edges.1 = (f32[2,16,64,128]{3,2,1,0:T(8,128)S(1)}, f32[2,16,2,128]{3,2,1,0:T(2,128)S(1)}, f32[2,16,2,128]{3,2,1,0:T(2,128)S(1)}, f32[2,2048]{1,0:T(2,128)S(1)}, f32[2,2048]{1,0:T(2,128)S(1)}) custom-call(f32[16,64,128]{2,1,0:T(8,128)S(1)} %copy-done, f32[16,64,128]{2,1,0:T(8,128)S(1)} %copy-done.2, f32[16,64,128]{2,1,0:T(8,128)S(1)} %copy-done.5, ...), custom_call_target="tpu_custom_call" | custom-call | tf_op jit(solution)/shard_map/edges/pallas_call | solution.py:306
  5.6 0.0 copy-start.4
  5.6 0.5 %collective-permute-start.5 = (f32[2,2048]{1,0:T(2,128)S(1)}, f32[2,2048]{1,0:T(2,128)S(1)}, u32[]{:S(2)}, u32[]{:S(2)}) collective-permute-start(f32[2,2048]{1,0:T(2,128)S(1)} %get-tuple-element.18), channel_id=1, source_target_pairs={{0,1},{1,2},{2,3},{3,0},{4,5},{5,6},{6,7},{7,4},{8,9},{9,10},{10,1... | collective-permute-start | bytes 49160 | tf_op jit(solution)/shard_map/ppermute | solution.py:326
  6.2 2.0 %collective-permute-start.6 = (f32[2,2048]{1,0:T(2,128)S(1)}, f32[2,2048]{1,0:T(2,128)S(1)}, u32[]{:S(2)}, u32[]{:S(2)}) collective-permute-start(f32[2,2048]{1,0:T(2,128)S(1)} %get-tuple-element.19), channel_id=1, source_target_pairs={{1,0},{2,1},{3,2},{0,3},{5,4},{6,5},{7,6},{4,7},{9,8},{10,9},{11,1... | collective-permute-start | bytes 49160 | tf_op jit(solution)/shard_map/ppermute | solution.py:326
  8.1 2.3 %collective-permute-start.3 = (f32[2,16,2,128]{3,2,1,0:T(2,128)S(1)}, f32[2,16,2,128]{3,2,1,0:T(2,128)S(1)}, u32[]{:S(2)}, u32[]{:S(2)}) collective-permute-start(f32[2,16,2,128]{3,2,1,0:T(2,128)S(1)} %get-tuple-element.16), channel_id=1, source_target_pairs={{0,4},{4,8},{8,12},{12,16},{16,20},{20,24},{24,28},{28,0},{1,5},{5... | collective-permute-start | bytes 98312 | tf_op jit(solution)/shard_map/ppermute | solution.py:326
  10.4 3.0 %collective-permute-start.4 = (f32[2,16,2,128]{3,2,1,0:T(2,128)S(1)}, f32[2,16,2,128]{3,2,1,0:T(2,128)S(1)}, u32[]{:S(2)}, u32[]{:S(2)}) collective-permute-start(f32[2,16,2,128]{3,2,1,0:T(2,128)S(1)} %get-tuple-element.17), channel_id=1, source_target_pairs={{4,0},{8,4},{12,8},{16,12},{20,16},{24,20},{28,24},{0,28},{5,1},{9... | collective-permute-start | bytes 98312 | tf_op jit(solution)/shard_map/ppermute | solution.py:326
  13.5 0.0 copy-done.10
  14.2 0.0 copy-done.1
  14.2 0.0 copy-done.3
  14.2 0.0 copy-done.7
  14.2 0.0 copy-done.8
  14.2 0.0 copy-done.9
  14.2 8.8 %gather.1 = (f32[512,128]{1,0:T(8,128)S(1)}, f32[512,128]{1,0:T(8,128)S(1)}, f32[8,160]{1,0:T(8,128)S(1)}) custom-call(s32[4096]{0:T(1024)S(1)} %bitcast.5, s32[4096]{0:T(1024)S(1)} %get-tuple-element.24.turn, s32[1,1]{1,0:T(1,128)S(6)} %copy.12.tally, f32[16,64,128]{2,1,0:T(8,128)S(1)} %copy-done.1, f32[16,64,128]{2,1,0:T(8,128)S(1)} %copy-done.3, ...), custom_call_target="tpu_custom_call" | custom-call | tf_op jit(solution)/shard_map/gather/pallas_call | solution.py:331
  23.0 0.1 collective-permute-start
  23.0 3.6 %collective-permute-done = f32[8,160]{1,0:T(8,128)S(1)} collective-permute-done((f32[8,160]{1,0:T(8,128)S(1)}, f32[8,160]{1,0:T(8,128)S(1)}, u32[]{:S(2)}, u32[]{:S(2)}) %collective-permute-start) | collective-permute-done | bytes 5152 | tf_op jit(solution)/shard_map/ppermute | solution.py:352
  26.7 0.0 collective-permute-start.1
  26.7 3.6 %collective-permute-done.1 = f32[8,160]{1,0:T(8,128)S(1)} collective-permute-done((f32[8,160]{1,0:T(8,128)S(1)}, f32[8,160]{1,0:T(8,128)S(1)}, u32[]{:S(2)}, u32[]{:S(2)}) %collective-permute-start.1) | collective-permute-done | bytes 5152 | tf_op jit(solution)/shard_map/ppermute | solution.py:352
  30.3 1.0 %collective-permute-start.2 = (f32[8,160]{1,0:T(8,128)S(1)}, f32[8,160]{1,0:T(8,128)S(1)}, u32[]{:S(2)}, u32[]{:S(2)}) collective-permute-start(f32[8,160]{1,0:T(8,128)S(1)} %add.22), channel_id=1, source_target_pairs={{0,16},{4,20},{8,24},{12,28},{16,0},{20,4},{24,8},{28,12},{1,17},{... | collective-permute-start | bytes 15368 | tf_op jit(solution)/shard_map/ppermute | solution.py:352
  31.3 3.6 %collective-permute-done.2 = f32[8,160]{1,0:T(8,128)S(1)} collective-permute-done((f32[8,160]{1,0:T(8,128)S(1)}, f32[8,160]{1,0:T(8,128)S(1)}, u32[]{:S(2)}, u32[]{:S(2)}) %collective-permute-start.2) | collective-permute-done | bytes 5152 | tf_op jit(solution)/shard_map/ppermute | solution.py:352
  34.9 0.0 collective-permute-done.5.left
  34.9 0.0 collective-permute-done.6.right
  34.9 0.0 collective-permute-done.3.above
  34.9 0.0 collective-permute-done.4.below
  34.9 0.0 copy-done.4
  34.9 2.8 %stencil.1 = (f32[16,64,128]{2,1,0:T(8,128)S(1)}, f32[16,64,128]{2,1,0:T(8,128)S(1)}) custom-call(f32[2,16,64,128]{3,2,1,0:T(8,128)S(1)} %get-tuple-element.15.blend, f32[16,64,128]{2,1,0:T(8,128)S(1)} %copy-done.1, f32[16,64,128]{2,1,0:T(8,128)S(1)} %copy-done.3, bf16[3,16,64,128]{3,2,1,0:T(8,128)(2,1)S(1)} %copy-done.4, ...), custom_call_target="tpu_custom_call" | custom-call | tf_op jit(solution)/shard_map/stencil/pallas_call | solution.py:354
  37.7 10.3 %scatter.1 = (f32[16,64,128]{2,1,0:T(8,128)}, f32[16,64,128]{2,1,0:T(8,128)}) custom-call(s32[4096]{0:T(1024)S(1)} %bitcast.6, s32[4096]{0:T(1024)S(1)} %get-tuple-element.25.turn, f32[512,128]{1,0:T(8,128)S(1)} %get-tuple-element.12.scaled, f32[512,128]{1,0:T(8,128)S(1)} %get-tuple-element.13.fronts, s32[32,128]{1,0:T(8,128)S(1)} %bitcast.9, ...), custom_call_target="tpu_custom_call" | custom-call | tf_op jit(solution)/shard_map/scatter/pallas_call | solution.py:368
  (5 shorter events, 0.1 us)
Async XLA Ops:
  0.6 1.0 %copy-start = (f32[16,64,128]{2,1,0:T(8,128)S(1)}, f32[16,64,128]{2,1,0:T(8,128)}, u32[]{:S(2)}) copy-start(f32[16,64,128]{2,1,0:T(8,128)} %moist.5) | copy-start | bytes 1572868
  1.7 1.0 %copy-start.2 = (f32[16,64,128]{2,1,0:T(8,128)S(1)}, f32[16,64,128]{2,1,0:T(8,128)}, u32[]{:S(2)}) copy-start(f32[16,64,128]{2,1,0:T(8,128)} %warm.5) | copy-start | bytes 1572868
  2.7 1.0 %copy-start.5 = (f32[16,64,128]{2,1,0:T(8,128)S(1)}, f32[16,64,128]{2,1,0:T(8,128)}, u32[]{:S(2)}) copy-start(f32[16,64,128]{2,1,0:T(8,128)} %old_moist.1) | copy-start | bytes 1572868
  3.8 1.0 %copy-start.6 = (f32[16,64,128]{2,1,0:T(8,128)S(1)}, f32[16,64,128]{2,1,0:T(8,128)}, u32[]{:S(2)}) copy-start(f32[16,64,128]{2,1,0:T(8,128)} %old_warm.1) | copy-start | bytes 1572868
  4.8 8.7 %copy-start.10 = (s32[3,1,4096]{2,1,0:T(1,128)S(1)}, s32[3,1,4096]{2,1,0:T(1,128)}, u32[]{:S(2)}) copy-start(s32[3,1,4096]{2,1,0:T(1,128)} %param.15) | copy-start | bytes 147460
  4.8 9.4 %copy-start.1 = (f32[16,64,128]{2,1,0:T(8,128)S(1)}, f32[16,64,128]{2,1,0:T(8,128)}, u32[]{:S(2)}) copy-start(f32[16,64,128]{2,1,0:T(8,128)} %moist.5) | copy-start | bytes 1572868
  4.8 9.4 %copy-start.3 = (f32[16,64,128]{2,1,0:T(8,128)S(1)}, f32[16,64,128]{2,1,0:T(8,128)}, u32[]{:S(2)}) copy-start(f32[16,64,128]{2,1,0:T(8,128)} %warm.5) | copy-start | bytes 1572868
  4.8 9.4 %copy-start.7 = (f32[8,1,4096]{2,1,0:T(1,128)S(1)}, f32[8,1,4096]{2,1,0:T(1,128)}, u32[]{:S(2)}) copy-start(f32[8,1,4096]{2,1,0:T(1,128)} %param.16) | copy-start | bytes 393220
  4.8 9.4 %copy-start.8 = (s32[1,4096]{1,0:T(1,128)S(1)}, s32[1,4096]{1,0:T(1,128)}, u32[]{:S(2)}) copy-start(s32[1,4096]{1,0:T(1,128)} %param.18) | copy-start | bytes 49156
  4.8 9.4 %copy-start.9 = (f32[1,4096]{1,0:T(1,128)S(1)}, f32[1,4096]{1,0:T(1,128)}, u32[]{:S(2)}) copy-start(f32[1,4096]{1,0:T(1,128)} %param.17) | copy-start | bytes 49156
  5.6 29.3 %copy-start.4 = (bf16[3,16,64,128]{3,2,1,0:T(8,128)(2,1)S(1)}, bf16[3,16,64,128]{3,2,1,0:T(8,128)(2,1)}, u32[]{:S(2)}) copy-start(bf16[3,16,64,128]{3,2,1,0:T(8,128)(2,1)} %speed.1) | copy-start | bytes 2359300
  5.6 29.3 %collective-permute-start.5 = (f32[2,2048]{1,0:T(2,128)S(1)}, f32[2,2048]{1,0:T(2,128)S(1)}, u32[]{:S(2)}, u32[]{:S(2)}) collective-permute-start(f32[2,2048]{1,0:T(2,128)S(1)} %get-tuple-element.18), channel_id=1, source_target_pairs={{0,1},{1,2},{2,3},{3,0},{4,5},{5,6},{6,7},{7,4},{8,9},{9,10},{10,1... | collective-permute-start | bytes 49160 | tf_op jit(solution)/shard_map/ppermute | solution.py:326
  6.2 28.8 %collective-permute-start.6 = (f32[2,2048]{1,0:T(2,128)S(1)}, f32[2,2048]{1,0:T(2,128)S(1)}, u32[]{:S(2)}, u32[]{:S(2)}) collective-permute-start(f32[2,2048]{1,0:T(2,128)S(1)} %get-tuple-element.19), channel_id=1, source_target_pairs={{1,0},{2,1},{3,2},{0,3},{5,4},{6,5},{7,6},{4,7},{9,8},{10,9},{11,1... | collective-permute-start | bytes 49160 | tf_op jit(solution)/shard_map/ppermute | solution.py:326
  8.1 26.8 %collective-permute-start.3 = (f32[2,16,2,128]{3,2,1,0:T(2,128)S(1)}, f32[2,16,2,128]{3,2,1,0:T(2,128)S(1)}, u32[]{:S(2)}, u32[]{:S(2)}) collective-permute-start(f32[2,16,2,128]{3,2,1,0:T(2,128)S(1)} %get-tuple-element.16), channel_id=1, source_target_pairs={{0,4},{4,8},{8,12},{12,16},{16,20},{20,24},{24,28},{28,0},{1,5},{5... | collective-permute-start | bytes 98312 | tf_op jit(solution)/shard_map/ppermute | solution.py:326
  10.4 24.5 %collective-permute-start.4 = (f32[2,16,2,128]{3,2,1,0:T(2,128)S(1)}, f32[2,16,2,128]{3,2,1,0:T(2,128)S(1)}, u32[]{:S(2)}, u32[]{:S(2)}) collective-permute-start(f32[2,16,2,128]{3,2,1,0:T(2,128)S(1)} %get-tuple-element.17), channel_id=1, source_target_pairs={{4,0},{8,4},{12,8},{16,12},{20,16},{24,20},{28,24},{0,28},{5,1},{9... | collective-permute-start | bytes 98312 | tf_op jit(solution)/shard_map/ppermute | solution.py:326
  23.0 3.7 %collective-permute-start = (f32[8,160]{1,0:T(8,128)S(1)}, f32[8,160]{1,0:T(8,128)S(1)}, u32[]{:S(2)}, u32[]{:S(2)}) collective-permute-start(f32[8,160]{1,0:T(8,128)S(1)} %get-tuple-element.14), channel_id=1, source_target_pairs={{0,4},{4,0},{8,12},{12,8},{16,20},{20,16},{24,28},{28,24},{1,5},{5... | collective-permute-start | bytes 15368 | tf_op jit(solution)/shard_map/ppermute | solution.py:352
  26.7 3.7 %collective-permute-start.1 = (f32[8,160]{1,0:T(8,128)S(1)}, f32[8,160]{1,0:T(8,128)S(1)}, u32[]{:S(2)}, u32[]{:S(2)}) collective-permute-start(f32[8,160]{1,0:T(8,128)S(1)} %add.21), channel_id=1, source_target_pairs={{0,8},{4,12},{8,0},{12,4},{16,24},{20,28},{24,16},{28,20},{1,9},{5... | collective-permute-start | bytes 15368 | tf_op jit(solution)/shard_map/ppermute | solution.py:352
  30.3 4.5 %collective-permute-start.2 = (f32[8,160]{1,0:T(8,128)S(1)}, f32[8,160]{1,0:T(8,128)S(1)}, u32[]{:S(2)}, u32[]{:S(2)}) collective-permute-start(f32[8,160]{1,0:T(8,128)S(1)} %add.22), channel_id=1, source_target_pairs={{0,16},{4,20},{8,24},{12,28},{16,0},{20,4},{24,8},{28,12},{1,17},{... | collective-permute-start | bytes 15368 | tf_op jit(solution)/shard_map/ppermute | solution.py:352

commit v3 on v2

--- a/solution.py
+++ b/solution.py
@@ -23,6 +23,7 @@
 SMEM = pl.BlockSpec(memory_space=pltpu.SMEM)
 COPIES = 4
 UNROLL = 4
+EDGES = 62
 
 
 def iota(shape, dim):
@@ -37,7 +38,7 @@
     return jnp.where(even, pltpu.roll(x, 7, 0), pltpu.roll(x, 1, 0))
 
 
-def edges_kernel(moist, warm, old_moist, old_warm, blend, top, bottom, left, right, stage, arrived):
+def edges_kernel(moist, warm, old_moist, old_warm, top, bottom, left, right, stage, arrived):
     planes, rows, cols = moist.shape
     parts = 2
     step = planes // parts
@@ -62,7 +63,6 @@
             halves = []
             for plane in (2 * pair, 2 * pair + 1):
                 mixed = 1.5 * stage[2 * field, plane] - 0.5 * stage[2 * field + 1, plane]
-                blend[field, plane] = mixed
                 top[field, plane] = mixed[0:2]
                 bottom[field, plane] = mixed[rows - 2 : rows]
                 halves.append(mixed)
@@ -150,16 +150,16 @@
     sums[...] = total[0:8] + total[8:16]
 
 
-def stencil_kernel(blend, moist, warm, speed, above, below, left, right, out_moist, out_warm, padded, side):
-    planes, rows, cols = moist.shape
-    for field in range(2):
+def prepare(fields, halos, padded, side):
+    above, below, left, right = halos
+    planes, rows, cols = fields[0][0].shape
+    for field, (now, old) in enumerate(fields):
         for plane in range(planes):
-            padded[field, plane, 8 : rows + 8, :] = blend[field, plane]
+            padded[field, plane, 8 : rows + 8, :] = 1.5 * now[plane] - 0.5 * old[plane]
             padded[field, plane, 6:8, :] = above[field, plane]
             padded[field, plane, rows + 8 : rows + 10, :] = below[field, plane]
         for pair in range(planes // 2):
-            slot = field * (planes // 2) + pair
-            at = slot * 2 * rows
+            at = (field * (planes // 2) + pair) * 2 * rows
             block = jnp.concatenate(
                 [
                     right[:, pl.ds(at, 2 * rows)],
@@ -168,45 +168,68 @@
                 ],
                 axis=0,
             )
-            side[pl.ds(slot * 2 * rows, 2 * rows), :] = block.T
+            side[pl.ds(at, 2 * rows), :] = block.T
+
+
+def advance(plane, fields, speed, padded, side, outs):
+    planes, rows, cols = fields[0][0].shape
     lane = iota((rows, cols), 1)
     fraction = increment_span / 12.0
-
-    def plane_step(plane, carry):
-        speeds = [speed[k, plane].astype(jnp.float32) * fraction for k in range(3)]
-        for field, (now, out) in enumerate(((moist, out_moist), (warm, out_warm))):
-            center = padded[field, plane, 8 : rows + 8, :]
-            edge = side[pl.ds(pl.multiple_of((field * planes + plane) * rows, rows), rows), :]
-            wrap = lambda shift: padded[field, lax.rem(plane + shift + planes, planes), 8 : rows + 8, :]
-            shift = lambda by: padded[field, plane, 8 + by : rows + 8 + by, :]
-            around = [
-                (wrap(1), wrap(2), wrap(-1), wrap(-2)),
-                (shift(1), shift(2), shift(-1), shift(-2)),
-                (
-                    pltpu.roll(jnp.where(lane < 1, edge, center), cols - 1, 1),
-                    pltpu.roll(jnp.where(lane < 2, edge, center), cols - 2, 1),
-                    pltpu.roll(jnp.where(lane >= cols - 1, edge, center), 1, 1),
-                    pltpu.roll(jnp.where(lane >= cols - 2, edge, center), 2, 1),
-                ),
-            ]
-            near = 0.0
-            far = 0.0
-            total = now[plane] - (90.0 * diffusivity * fraction) * center
-            for k, (ahead_one, ahead_two, behind_one, behind_two) in enumerate(around):
-                near = near + (ahead_one + behind_one)
-                far = far + (ahead_two + behind_two)
-                total = total - speeds[k] * (8.0 * (ahead_one - behind_one) - (ahead_two - behind_two))
-            out[plane] = total + (diffusivity * fraction) * (16.0 * near - far)
-        return carry
-
-    lax.fori_loop(0, planes, plane_step, 0)
-
-
-def scatter_kernel(begin, turn, scaled, fronts, owner, sums, start_moist, start_warm, out_moist, out_warm, *banks):
-    planes, rows, cols = start_moist.shape
+    speeds = [speed[k, plane].astype(jnp.float32) * fraction for k in range(3)]
+    for field in range(2):
+        center = padded[field, plane, 8 : rows + 8, :]
+        edge = side[pl.ds(pl.multiple_of((field * planes + plane) * rows, rows), rows), :]
+        wrap = lambda shift: padded[field, lax.rem(plane + shift + planes, planes), 8 : rows + 8, :]
+        shift = lambda by: padded[field, plane, 8 + by : rows + 8 + by, :]
+        around = [
+            (wrap(1), wrap(2), wrap(-1), wrap(-2)),
+            (shift(1), shift(2), shift(-1), shift(-2)),
+            (
+                pltpu.roll(jnp.where(lane < 1, edge, center), cols - 1, 1),
+                pltpu.roll(jnp.where(lane < 2, edge, center), cols - 2, 1),
+                pltpu.roll(jnp.where(lane >= cols - 1, edge, center), 1, 1),
+                pltpu.roll(jnp.where(lane >= cols - 2, edge, center), 2, 1),
+            ),
+        ]
+        near = 0.0
+        far = 0.0
+        total = fields[field][0][plane] - (90.0 * diffusivity * fraction) * center
+        for k, (ahead_one, ahead_two, behind_one, behind_two) in enumerate(around):
+            near = near + (ahead_one + behind_one)
+            far = far + (ahead_two + behind_two)
+            total = total - speeds[k] * (8.0 * (ahead_one - behind_one) - (ahead_two - behind_two))
+        outs[field][plane] = total + (diffusivity * fraction) * (16.0 * near - far)
+
+
+def scatter_kernel(
+    begin,
+    turn,
+    scaled,
+    fronts,
+    owner,
+    sums,
+    moist,
+    warm,
+    old_moist,
+    old_warm,
+    speed,
+    above,
+    below,
+    left,
+    right,
+    out_moist,
+    out_warm,
+    padded,
+    side,
+    *banks,
+):
+    planes, rows, cols = moist.shape
     groups = owner.shape[0]
     drops = sums.shape[1]
     size = banks[0].shape[0]
+    fields = ((moist, old_moist), (warm, old_warm))
+    outs = (out_moist, out_warm)
+    prepare(fields, (above, below, left, right), padded, side)
 
     def clear(step, carry):
         for bank in banks:
@@ -253,18 +276,24 @@
                 entry = jnp.where((lane >> 1) == j, values[half], 0.0)
                 banks[j % len(banks)][pl.ds(begin[at], 8), :] += pltpu.roll(entry, turn[at], 1)
 
+    def grid_share(block):
+        for number in range(planes // count):
+            advance(block * (planes // count) + number, fields, speed, padded, side, outs)
+
     def step(block, values):
         later = ready(block + 1)
+        grid_share(block)
         spill(block, values)
         return tuple(later)
 
     count = groups // UNROLL
     values = lax.fori_loop(0, count - 1, step, tuple(ready(0)))
+    grid_share(count - 1)
     spill(count - 1, values)
     for plane in range(planes):
         before = (plane - 1) % planes
-        for field, (start, out) in enumerate(((start_moist, out_moist), (start_warm, out_warm))):
-            total = start[plane]
+        for field, out in enumerate(outs):
+            total = out[plane]
             for bank in banks:
                 total = total + bank[pl.ds(plane * rows * 4 + field, rows, stride=4), :]
                 total = total + bank[pl.ds(before * rows * 4 + 2 + field, rows, stride=4), :]
@@ -303,19 +332,18 @@
     owner = panel_owner.reshape(groups, LANES)
     field = shape((planes, rows, cols), f32)
 
-    blend, top, bottom, left, right = pl.pallas_call(
+    top, bottom, left, right = pl.pallas_call(
         edges_kernel,
         out_shape=(
-            shape((2, planes, rows, cols), f32),
             shape((2, planes, 2, cols), f32),
             shape((2, planes, 2, cols), f32),
             shape((2, 2 * planes * rows), f32),
             shape((2, 2 * planes * rows), f32),
         ),
         in_specs=[HBM] * 4,
-        out_specs=[VMEM] * 5,
+        out_specs=[VMEM] * 4,
         scratch_shapes=[pltpu.VMEM((4, planes, rows, cols), f32), pltpu.SemaphoreType.DMA((8,))],
-        compiler_params=params(),
+        compiler_params=params(EDGES),
         name="edges",
     )(gas_moisture, gas_warmth, prior_moisture, prior_warmth)
 
@@ -351,29 +379,36 @@
             swap = [(i, i ^ (1 << bit)) for i in range(size)]
             totals = totals + lax.ppermute(totals, "gx", swap)
 
-    start_moist, start_warm = pl.pallas_call(
-        stencil_kernel,
+    size = planes * rows * 4 + 128
+    return pl.pallas_call(
+        scatter_kernel,
         out_shape=(field, field),
-        in_specs=[VMEM] * 8,
+        in_specs=[SMEM] * 2 + [VMEM] * 13,
         out_specs=[VMEM] * 2,
         scratch_shapes=[
             pltpu.VMEM((2, planes, rows + 16, cols), f32),
             pltpu.VMEM((2 * planes * rows, cols), f32),
-        ],
-        compiler_params=params(),
-        name="stencil",
-    )(blend, gas_moisture, gas_warmth, flow_speeds, above, below, from_left, from_right)
-
-    size = planes * rows * 4 + 128
-    return pl.pallas_call(
-        scatter_kernel,
-        out_shape=(field, field),
-        in_specs=[SMEM] * 2 + [VMEM] * 6,
-        out_specs=[VMEM] * 2,
-        scratch_shapes=[pltpu.VMEM((size, cols), f32)] * COPIES,
+        ]
+        + [pltpu.VMEM((size, cols), f32)] * COPIES,
         compiler_params=params(),
         name="scatter",
-    )(start, back, scaled, fronts, owner, totals, start_moist, start_warm)
+    )(
+        start,
+        back,
+        scaled,
+        fronts,
+        owner,
+        totals,
+        gas_moisture,
+        gas_warmth,
+        prior_moisture,
+        prior_warmth,
+        flow_speeds,
+        above,
+        below,
+        from_left,
+        from_right,
+    )
 
 
 def solution(mesh):

time: 48.3 us -> 44.2 us (0.915)
  local copies, waits for them, and re-layouts: 4.19 us -> 0.05 us
    unnamed x22 -> x18, local copies, waits for them, and re-layouts: 4.19 us -> 0.05 us
    pallas_call x1, Pallas kernels: 10.3 us -> 11.5 us  [shards(): pl.pallas_call(scatter_kernel, out_shape=(field, field), in_specs=[SMEM]...]
    pallas_call x2 -> x1, Pallas kernels: 3.55 us -> 2.44 us  [shards(): pl.pallas_call(edges_kernel, out_shape=(shape((2, planes, 2, cols), f32),...]
  transfers between devices with their start and end apart: 7 -> 7, of which waited for: 3 -> 3; matrix products, arithmetic and copies ran while one was open for 0% -> 0% of each run, Pallas kernels for 18% -> 20%
where the time goes in v3:
time: 44.2 us; the launch traced here: 44 us
  Pallas kernels  22.7 us (51%)
  waiting for transfers between devices  10.9 us (25%)
  starting transfers between devices  8.81 us (20%)
  between operations  1.46 us (3%)
    pallas_call x1, Pallas kernels, shards(): pl.pallas_call(scatter_kernel, out_shape=(field, field), in_specs=[SMEM]...  11.5 us
    ppermute x3, waiting for transfers between devices, shards(): totals = totals + lax.ppermute(totals, 'gx', swap)  10.9 us
    pallas_call x1, Pallas kernels, shards(): pl.pallas_call(gather_kernel, out_shape=(shape((2 * groups * 8, LANES), f...  8.77 us
    ppermute x2, starting transfers between devices, around(): lax.ppermute(head, axis, backward)  5.03 us
    ppermute x2, starting transfers between devices, around(): lax.ppermute(tail, axis, onward)  2.77 us
    pallas_call x1, Pallas kernels, shards(): pl.pallas_call(edges_kernel, out_shape=(shape((2, planes, 2, cols), f32),...  2.44 us
    ppermute x3, starting transfers between devices, shards(): totals = totals + lax.ppermute(totals, 'gx', swap)  1.01 us
  transfers between devices with their start and end apart: 7, of which 3 were waited for; matrix products, arithmetic and copies ran while one was open for 0% of the time, Pallas kernels for 20%

profile of v3, /device:TPU:0, one launch (start us, length us, event | category | flops | bytes accessed | tf_op | source)
XLA Modules:
  0.0 44.0 jit_solution(13986553228405489346)
XLA Ops:
  0.6 0.0 copy-start.8
  0.6 0.0 copy-start
  0.7 0.0 copy-start.1
  0.7 0.0 copy-start.4
  0.7 2.4 %edges.1 = (f32[2,16,2,128]{3,2,1,0:T(2,128)}, f32[2,16,2,128]{3,2,1,0:T(2,128)}, f32[2,2048]{1,0:T(2,128)}, f32[2,2048]{1,0:T(2,128)}) custom-call(f32[16,64,128]{2,1,0:T(8,128)} %moist.5, f32[16,64,128]{2,1,0:T(8,128)} %warm.5, f32[16,64,128]{2,1,0:T(8,128)} %old_moist.3, f32[16,64,128]{2,1,0:T(8,128)} %old_warm.3), custom_call_target="tpu_custom_call" | custom-call | tf_op jit(solution)/shard_map/edges/pallas_call | solution.py:335
  3.1 0.0 copy-start.5
  3.1 0.5 %collective-permute-start.5 = (f32[2,2048]{1,0:T(2,128)}, f32[2,2048]{1,0:T(2,128)S(1)}, u32[]{:S(2)}, u32[]{:S(2)}) collective-permute-start(f32[2,2048]{1,0:T(2,128)} %get-tuple-element.14), channel_id=1, source_target_pairs={{0,1},{1,2},{2,3},{3,0},{4,5},{5,6},{6,7},{7,4},{8,9},{9,10},{10,1... | collective-permute-start | bytes 49160 | tf_op jit(solution)/shard_map/ppermute | solution.py:354
  3.6 2.0 %collective-permute-start.6 = (f32[2,2048]{1,0:T(2,128)}, f32[2,2048]{1,0:T(2,128)S(1)}, u32[]{:S(2)}, u32[]{:S(2)}) collective-permute-start(f32[2,2048]{1,0:T(2,128)} %get-tuple-element.15), channel_id=1, source_target_pairs={{1,0},{2,1},{3,2},{0,3},{5,4},{6,5},{7,6},{4,7},{9,8},{10,9},{11,1... | collective-permute-start | bytes 49160 | tf_op jit(solution)/shard_map/ppermute | solution.py:354
  5.6 2.3 %collective-permute-start.3 = (f32[2,16,2,128]{3,2,1,0:T(2,128)}, f32[2,16,2,128]{3,2,1,0:T(2,128)S(1)}, u32[]{:S(2)}, u32[]{:S(2)}) collective-permute-start(f32[2,16,2,128]{3,2,1,0:T(2,128)} %get-tuple-element.12), channel_id=1, source_target_pairs={{0,4},{4,8},{8,12},{12,16},{16,20},{20,24},{24,28},{28,0},{1,5},{5... | collective-permute-start | bytes 98312 | tf_op jit(solution)/shard_map/ppermute | solution.py:354
  7.9 3.0 %collective-permute-start.4 = (f32[2,16,2,128]{3,2,1,0:T(2,128)}, f32[2,16,2,128]{3,2,1,0:T(2,128)S(1)}, u32[]{:S(2)}, u32[]{:S(2)}) collective-permute-start(f32[2,16,2,128]{3,2,1,0:T(2,128)} %get-tuple-element.13), channel_id=1, source_target_pairs={{4,0},{8,4},{12,8},{16,12},{20,16},{24,20},{28,24},{0,28},{5,1},{9... | collective-permute-start | bytes 98312 | tf_op jit(solution)/shard_map/ppermute | solution.py:354
  10.9 0.0 copy-done.8
  11.0 0.0 copy-start.6
  11.0 0.0 copy-start.7
  11.7 0.0 copy-done
  11.7 0.0 copy-done.1
  11.7 0.0 copy-done.5
  11.7 0.0 copy-done.6
  11.7 0.0 copy-done.7
  11.7 0.0 copy-start.2
  11.7 0.0 copy-start.3
  11.7 8.8 %gather.1 = (f32[512,128]{1,0:T(8,128)S(1)}, f32[512,128]{1,0:T(8,128)S(1)}, f32[8,160]{1,0:T(8,128)S(1)}) custom-call(s32[4096]{0:T(1024)S(1)} %bitcast.5, s32[4096]{0:T(1024)S(1)} %get-tuple-element.18.turn, s32[1,1]{1,0:T(1,128)S(6)} %copy.12.tally, f32[16,64,128]{2,1,0:T(8,128)S(1)} %copy-done, f32[16,64,128]{2,1,0:T(8,128)S(1)} %copy-done.1, ...), custom_call_target="tpu_custom_call" | custom-call | tf_op jit(solution)/shard_map/gather/pallas_call | solution.py:359
  20.5 0.1 collective-permute-start
  20.6 3.6 %collective-permute-done = f32[8,160]{1,0:T(8,128)S(1)} collective-permute-done((f32[8,160]{1,0:T(8,128)S(1)}, f32[8,160]{1,0:T(8,128)S(1)}, u32[]{:S(2)}, u32[]{:S(2)}) %collective-permute-start) | collective-permute-done | bytes 5152 | tf_op jit(solution)/shard_map/ppermute | solution.py:380
  24.2 0.0 collective-permute-start.1
  24.2 3.6 %collective-permute-done.1 = f32[8,160]{1,0:T(8,128)S(1)} collective-permute-done((f32[8,160]{1,0:T(8,128)S(1)}, f32[8,160]{1,0:T(8,128)S(1)}, u32[]{:S(2)}, u32[]{:S(2)}) %collective-permute-start.1) | collective-permute-done | bytes 5152 | tf_op jit(solution)/shard_map/ppermute | solution.py:380
  27.9 1.0 %collective-permute-start.2 = (f32[8,160]{1,0:T(8,128)S(1)}, f32[8,160]{1,0:T(8,128)S(1)}, u32[]{:S(2)}, u32[]{:S(2)}) collective-permute-start(f32[8,160]{1,0:T(8,128)S(1)} %add.22), channel_id=1, source_target_pairs={{0,16},{4,20},{8,24},{12,28},{16,0},{20,4},{24,8},{28,12},{1,17},{... | collective-permute-start | bytes 15368 | tf_op jit(solution)/shard_map/ppermute | solution.py:380
  28.8 3.6 %collective-permute-done.2 = f32[8,160]{1,0:T(8,128)S(1)} collective-permute-done((f32[8,160]{1,0:T(8,128)S(1)}, f32[8,160]{1,0:T(8,128)S(1)}, u32[]{:S(2)}, u32[]{:S(2)}) %collective-permute-start.2) | collective-permute-done | bytes 5152 | tf_op jit(solution)/shard_map/ppermute | solution.py:380
  32.4 0.0 collective-permute-done.5.left
  32.4 0.0 collective-permute-done.6.right
  32.4 0.0 collective-permute-done.3.above
  32.4 0.0 collective-permute-done.4.below
  32.5 0.0 copy-done.4
  32.5 0.0 copy-done.2
  32.5 0.0 copy-done.3
  32.5 11.5 %scatter.1 = (f32[16,64,128]{2,1,0:T(8,128)}, f32[16,64,128]{2,1,0:T(8,128)}) custom-call(s32[4096]{0:T(1024)S(1)} %bitcast.6, s32[4096]{0:T(1024)S(1)} %get-tuple-element.19.turn, f32[512,128]{1,0:T(8,128)S(1)} %get-tuple-element.9.scaled, f32[512,128]{1,0:T(8,128)S(1)} %get-tuple-element.10.fronts, s32[32,128]{1,0:T(8,128)S(1)} %bitcast.9, ...), custom_call_target="tpu_custom_call" | custom-call | tf_op jit(solution)/shard_map/scatter/pallas_call | solution.py:383
  (5 shorter events, 0.1 us)
Async XLA Ops:
  0.6 10.3 %copy-start.8 = (s32[3,1,4096]{2,1,0:T(1,128)S(1)}, s32[3,1,4096]{2,1,0:T(1,128)}, u32[]{:S(2)}) copy-start(s32[3,1,4096]{2,1,0:T(1,128)} %param.15) | copy-start | bytes 147460
  0.6 11.0 %copy-start = (f32[16,64,128]{2,1,0:T(8,128)S(1)}, f32[16,64,128]{2,1,0:T(8,128)}, u32[]{:S(2)}) copy-start(f32[16,64,128]{2,1,0:T(8,128)} %moist.5) | copy-start | bytes 1572868
  0.7 11.0 %copy-start.1 = (f32[16,64,128]{2,1,0:T(8,128)S(1)}, f32[16,64,128]{2,1,0:T(8,128)}, u32[]{:S(2)}) copy-start(f32[16,64,128]{2,1,0:T(8,128)} %warm.5) | copy-start | bytes 1572868
  0.7 31.8 %copy-start.4 = (bf16[3,16,64,128]{3,2,1,0:T(8,128)(2,1)S(1)}, bf16[3,16,64,128]{3,2,1,0:T(8,128)(2,1)}, u32[]{:S(2)}) copy-start(bf16[3,16,64,128]{3,2,1,0:T(8,128)(2,1)} %speed.1) | copy-start | bytes 2359300
  3.1 8.6 %copy-start.5 = (f32[8,1,4096]{2,1,0:T(1,128)S(1)}, f32[8,1,4096]{2,1,0:T(1,128)}, u32[]{:S(2)}) copy-start(f32[8,1,4096]{2,1,0:T(1,128)} %param.16) | copy-start | bytes 393220
  3.1 29.3 %collective-permute-start.5 = (f32[2,2048]{1,0:T(2,128)}, f32[2,2048]{1,0:T(2,128)S(1)}, u32[]{:S(2)}, u32[]{:S(2)}) collective-permute-start(f32[2,2048]{1,0:T(2,128)} %get-tuple-element.14), channel_id=1, source_target_pairs={{0,1},{1,2},{2,3},{3,0},{4,5},{5,6},{6,7},{7,4},{8,9},{9,10},{10,1... | collective-permute-start | bytes 49160 | tf_op jit(solution)/shard_map/ppermute | solution.py:354
  3.6 28.8 %collective-permute-start.6 = (f32[2,2048]{1,0:T(2,128)}, f32[2,2048]{1,0:T(2,128)S(1)}, u32[]{:S(2)}, u32[]{:S(2)}) collective-permute-start(f32[2,2048]{1,0:T(2,128)} %get-tuple-element.15), channel_id=1, source_target_pairs={{1,0},{2,1},{3,2},{0,3},{5,4},{6,5},{7,6},{4,7},{9,8},{10,9},{11,1... | collective-permute-start | bytes 49160 | tf_op jit(solution)/shard_map/ppermute | solution.py:354
  5.6 26.8 %collective-permute-start.3 = (f32[2,16,2,128]{3,2,1,0:T(2,128)}, f32[2,16,2,128]{3,2,1,0:T(2,128)S(1)}, u32[]{:S(2)}, u32[]{:S(2)}) collective-permute-start(f32[2,16,2,128]{3,2,1,0:T(2,128)} %get-tuple-element.12), channel_id=1, source_target_pairs={{0,4},{4,8},{8,12},{12,16},{16,20},{20,24},{24,28},{28,0},{1,5},{5... | collective-permute-start | bytes 98312 | tf_op jit(solution)/shard_map/ppermute | solution.py:354
  7.9 24.6 %collective-permute-start.4 = (f32[2,16,2,128]{3,2,1,0:T(2,128)}, f32[2,16,2,128]{3,2,1,0:T(2,128)S(1)}, u32[]{:S(2)}, u32[]{:S(2)}) collective-permute-start(f32[2,16,2,128]{3,2,1,0:T(2,128)} %get-tuple-element.13), channel_id=1, source_target_pairs={{4,0},{8,4},{12,8},{16,12},{20,16},{24,20},{28,24},{0,28},{5,1},{9... | collective-permute-start | bytes 98312 | tf_op jit(solution)/shard_map/ppermute | solution.py:354
  11.0 0.7 %copy-start.6 = (s32[1,4096]{1,0:T(1,128)S(1)}, s32[1,4096]{1,0:T(1,128)}, u32[]{:S(2)}) copy-start(s32[1,4096]{1,0:T(1,128)} %param.18) | copy-start | bytes 49156
  11.0 0.7 %copy-start.7 = (f32[1,4096]{1,0:T(1,128)S(1)}, f32[1,4096]{1,0:T(1,128)}, u32[]{:S(2)}) copy-start(f32[1,4096]{1,0:T(1,128)} %param.17) | copy-start | bytes 49156
  11.7 20.7 %copy-start.2 = (f32[16,64,128]{2,1,0:T(8,128)S(1)}, f32[16,64,128]{2,1,0:T(8,128)}, u32[]{:S(2)}) copy-start(f32[16,64,128]{2,1,0:T(8,128)} %old_moist.3) | copy-start | bytes 1572868
  11.7 20.7 %copy-start.3 = (f32[16,64,128]{2,1,0:T(8,128)S(1)}, f32[16,64,128]{2,1,0:T(8,128)}, u32[]{:S(2)}) copy-start(f32[16,64,128]{2,1,0:T(8,128)} %old_warm.3) | copy-start | bytes 1572868
  20.5 3.7 %collective-permute-start = (f32[8,160]{1,0:T(8,128)S(1)}, f32[8,160]{1,0:T(8,128)S(1)}, u32[]{:S(2)}, u32[]{:S(2)}) collective-permute-start(f32[8,160]{1,0:T(8,128)S(1)} %get-tuple-element.11), channel_id=1, source_target_pairs={{0,4},{4,0},{8,12},{12,8},{16,20},{20,16},{24,28},{28,24},{1,5},{5... | collective-permute-start | bytes 15368 | tf_op jit(solution)/shard_map/ppermute | solution.py:380
  24.2 3.7 %collective-permute-start.1 = (f32[8,160]{1,0:T(8,128)S(1)}, f32[8,160]{1,0:T(8,128)S(1)}, u32[]{:S(2)}, u32[]{:S(2)}) collective-permute-start(f32[8,160]{1,0:T(8,128)S(1)} %add.21), channel_id=1, source_target_pairs={{0,8},{4,12},{8,0},{12,4},{16,24},{20,28},{24,16},{28,20},{1,9},{5... | collective-permute-start | bytes 15368 | tf_op jit(solution)/shard_map/ppermute | solution.py:380
  27.9 4.5 %collective-permute-start.2 = (f32[8,160]{1,0:T(8,128)S(1)}, f32[8,160]{1,0:T(8,128)S(1)}, u32[]{:S(2)}, u32[]{:S(2)}) collective-permute-start(f32[8,160]{1,0:T(8,128)S(1)} %add.22), channel_id=1, source_target_pairs={{0,16},{4,20},{8,24},{12,28},{16,0},{20,4},{24,8},{28,12},{1,17},{... | collective-permute-start | bytes 15368 | tf_op jit(solution)/shard_map/ppermute | solution.py:380

commit v4 on v3

--- a/solution.py
+++ b/solution.py
@@ -23,7 +23,9 @@
 SMEM = pl.BlockSpec(memory_space=pltpu.SMEM)
 COPIES = 4
 UNROLL = 4
-EDGES = 62
+GATHER_MB = 53.85
+SCATTER_MB = 53.65
+PARTS = 4
 
 
 def iota(shape, dim):
@@ -38,52 +40,124 @@
     return jnp.where(even, pltpu.roll(x, 7, 0), pltpu.roll(x, 1, 0))
 
 
-def edges_kernel(moist, warm, old_moist, old_warm, top, bottom, left, right, stage, arrived):
-    planes, rows, cols = moist.shape
-    parts = 2
-    step = planes // parts
-    copies = []
-    for field, (now, old) in enumerate(((moist, old_moist), (warm, old_warm))):
-        for part in range(parts):
-            span = pl.ds(part * step, step)
-            row = []
-            for level, source in enumerate((now, old)):
-                slot = (field * parts + part) * 2 + level
-                row.append(
-                    pltpu.make_async_copy(
-                        source.at[span], stage.at[2 * field + level, span], arrived.at[slot]
-                    )
-                )
-                row[-1].start()
-            copies.append((field, part, row))
-    for field, part, row in copies:
-        for copy in row:
-            copy.wait()
-        for pair in range(part * step // 2, (part + 1) * step // 2):
-            halves = []
-            for plane in (2 * pair, 2 * pair + 1):
-                mixed = 1.5 * stage[2 * field, plane] - 0.5 * stage[2 * field + 1, plane]
-                top[field, plane] = mixed[0:2]
-                bottom[field, plane] = mixed[rows - 2 : rows]
-                halves.append(mixed)
-            turned = jnp.concatenate(halves, axis=0).T
-            at = (field * planes // 2 + pair) * 2 * rows
-            left[:, pl.ds(at, 2 * rows)] = turned[0:2]
-            right[:, pl.ds(at, 2 * rows)] = turned[cols - 2 : cols]
-
-
-def gather_kernel(start, turn, tally, moist, warm, factors, surface, owner, scaled, fronts, sums, table):
+def odd_row():
+    return (lax.axis_index("gx") & 1) == 1
+
+
+def fetch(source, target, arrived, slots):
+    copy = pltpu.make_async_copy(source, target, arrived.at[slots.pop()])
+    copy.start()
+    return copy
+
+
+def gather_kernel(
+    base_in,
+    tally_in,
+    moist,
+    warm,
+    old_moist,
+    old_warm,
+    factors_in,
+    surface_in,
+    owner_in,
+    start_out,
+    back_out,
+    owner_out,
+    scaled_out,
+    fronts_out,
+    sums,
+    facing,
+    backing,
+    head,
+    tail,
+    base,
+    tally,
+    factors,
+    surface,
+    owner,
+    table,
+    stage,
+    scaled,
+    fronts,
+    places,
+    start,
+    turn,
+    arrived,
+):
     planes, rows, cols = moist.shape
     groups = surface.shape[0]
-    drops = sums.shape[1]
+    count = groups // UNROLL
+    head_rows = facing.shape[0] - backing.shape[0]
+    step_planes = planes // PARTS
+    slots = list(range(arrived.shape[0]))
+    first = fetch(base_in, base, arrived, slots)
+    copies = []
+    for levels in ((0, 2), (1, 3)):
+        for part in range(PARTS):
+            for level in levels:
+                span = pl.ds(part * step_planes, step_planes)
+                source = (moist, old_moist, warm, old_warm)[level]
+                copies.append(fetch(source.at[span], stage.at[level, span], arrived, slots))
+    small = [
+        fetch(source, target, arrived, slots)
+        for source, target in (
+            (factors_in, factors),
+            (surface_in, surface),
+            (owner_in, owner),
+            (tally_in, tally),
+        )
+    ]
+    first.wait()
+    spot = (groups, LANES)
+    column = base[2 * groups : 3 * groups, :] - lax.axis_index("gy") * cols
+    twist = (2 * (iota(spot, 1) & (HALF - 1)) - column) & 127
+    row = base[groups : 2 * groups, :] - lax.axis_index("gx") * rows
+    places[0] = (base[0:groups, :] * rows + row) * 4
+    places[1] = twist
+    places[2] = (128 - twist) & 127
+    indices = [fetch(places.at[0], start, arrived, slots), fetch(places.at[1], turn, arrived, slots)]
+    results = [
+        fetch(places.at[0], start_out, arrived, slots),
+        fetch(places.at[2], back_out, arrived, slots),
+    ]
+    facing[0:head_rows, :] = jnp.zeros((head_rows, LANES), jnp.float32)
+    sums[...] = jnp.zeros(sums.shape, jnp.float32)
     for plane in range(planes):
+        if plane % step_planes == 0:
+            copies[plane // step_planes * 2].wait()
+            copies[plane // step_planes * 2 + 1].wait()
         below = (plane - 1) % planes
-        table[pl.ds(plane * rows * 4, rows, stride=4), :] = moist[plane]
-        table[pl.ds(plane * rows * 4 + 1, rows, stride=4), :] = warm[plane]
-        table[pl.ds(below * rows * 4 + 2, rows, stride=4), :] = moist[plane]
-        table[pl.ds(below * rows * 4 + 3, rows, stride=4), :] = warm[plane]
-    live = tally[0, 0]
+        table[pl.ds(plane * rows * 4, rows, stride=4), :] = stage[0, plane]
+        table[pl.ds(plane * rows * 4 + 1, rows, stride=4), :] = stage[2, plane]
+        table[pl.ds(below * rows * 4 + 2, rows, stride=4), :] = stage[0, plane]
+        table[pl.ds(below * rows * 4 + 3, rows, stride=4), :] = stage[2, plane]
+    for copy in copies[2 * PARTS :] + indices + small:
+        copy.wait()
+    results.append(fetch(owner, owner_out, arrived, slots))
+    odd = odd_row()
+    drops = DROP_DEV * lax.axis_size("gx")
+
+    def edges(block):
+        share = planes // 2 // count
+        for number in range(share):
+            for field in range(2):
+                pair = block * share + number
+                halves = []
+                for half in range(2):
+                    plane = pair * 2 + half
+                    mixed = 1.5 * stage[2 * field, plane] - 0.5 * stage[2 * field + 1, plane]
+                    top, bottom = mixed[0:2], mixed[rows - 2 : rows]
+                    at = (field * planes + plane) * 2
+                    facing[pl.ds(head_rows + at, 2), :] = jnp.where(odd, top, bottom)
+                    backing[pl.ds(at, 2), :] = jnp.where(odd, bottom, top)
+                    halves.append(mixed)
+                turned = jnp.concatenate(halves, axis=0).T
+                at = pl.multiple_of((field * (planes // 2) + pair) * 2 * rows, 2 * rows)
+                head[:, pl.ds(at, 2 * rows)] = turned[0:2]
+                tail[:, pl.ds(at, 2 * rows)] = turned[cols - 2 : cols]
+
     lane = iota((8, LANES), 1)
+    live = jnp.broadcast_to(tally[...], (8, LANES))
     sub = iota((8, LANES), 0)
     even = (sub & 1) == 0
     even_lane = (lane & 1) == 0
@@ -93,7 +167,7 @@
         for half in range(2 * UNROLL):
             found = jnp.zeros((8, LANES), jnp.float32)
             for j in range(HALF):
-                at = block * (UNROLL * LANES) + half * HALF + j
+                at = (block * UNROLL + half // 2, half % 2 * HALF + j)
                 entry = pltpu.roll(table[pl.ds(start[at], 8), :], turn[at], 1)
                 found = jnp.where(lane >= 2 * j, entry, found)
             blocks.append(found)
@@ -138,26 +212,57 @@
             preferred_element_type=jnp.float32,
         )
 
+    tray = UNROLL * 16
+    outward = [arrived.at[slots.pop()] for number in range(2)]
+
+    def sends(block):
+        span = pl.ds(pl.multiple_of(block * tray, tray), tray)
+        return [
+            pltpu.make_async_copy(scaled.at[span], scaled_out.at[span], outward[0]),
+            pltpu.make_async_copy(fronts.at[span], fronts_out.at[span], outward[1]),
+        ]
+
+    def send(block):
+        for copy in sends(block):
+            copy.start()
+
     def step(block, carry):
         total, *blocks = carry
         later = raw(block)
-        return (refine(block - 1, blocks, total), *later)
-
-    count = groups // UNROLL
+        edges(block - 1)
+        total = refine(block - 1, blocks, total)
+        send(block - 1)
+        return (total, *later)
+
     carry = (jnp.zeros((16, drops), jnp.float32), *raw(0))
     total, *blocks = lax.fori_loop(1, count, step, carry)
+    edges(count - 1)
     total = refine(count - 1, blocks, total)
-    sums[...] = total[0:8] + total[8:16]
+    send(count - 1)
+    total = total[0:8] + total[8:16]
+    for number, at in enumerate(range(0, drops, LANES)):
+        size = min(LANES, drops - at)
+        facing[8 * number : 8 * number + 8, 0:size] = total[:, at : at + size]
+        sums[8 * number : 8 * number + 8, 0:size] = total[:, at : at + size]
+    for copy in results:
+        copy.wait()
+    pltpu.make_async_copy(scaled, scaled_out, outward[0]).wait()
+    pltpu.make_async_copy(fronts, fronts_out, outward[1]).wait()
 
 
 def prepare(fields, halos, padded, side):
-    above, below, left, right = halos
+    facing, backing, left, right = halos
     planes, rows, cols = fields[0][0].shape
+    head_rows = facing.shape[0] - backing.shape[0]
+    odd = odd_row()
     for field, (now, old) in enumerate(fields):
         for plane in range(planes):
             padded[field, plane, 8 : rows + 8, :] = 1.5 * now[plane] - 0.5 * old[plane]
-            padded[field, plane, 6:8, :] = above[field, plane]
-            padded[field, plane, rows + 8 : rows + 10, :] = below[field, plane]
+            at = (field * planes + plane) * 2
+            near = facing[head_rows + at : head_rows + at + 2, :]
+            far = backing[at : at + 2, :]
+            padded[field, plane, 6:8, :] = jnp.where(odd, near, far)
+            padded[field, plane, rows + 8 : rows + 10, :] = jnp.where(odd, far, near)
         for pair in range(planes // 2):
             at = (field * (planes // 2) + pair) * 2 * rows
             block = jnp.concatenate(
@@ -202,34 +307,51 @@
 
 
 def scatter_kernel(
-    begin,
-    turn,
-    scaled,
-    fronts,
+    start_in,
+    back_in,
+    scaled_in,
+    fronts_in,
     owner,
     sums,
     moist,
     warm,
     old_moist,
     old_warm,
-    speed,
-    above,
-    below,
+    speed_in,
+    facing,
+    backing,
     left,
     right,
     out_moist,
     out_warm,
     padded,
     side,
+    stage,
+    speed,
+    scaled,
+    fronts,
+    result,
+    begin,
+    turn,
+    arrived,
     *banks,
 ):
     planes, rows, cols = moist.shape
     groups = owner.shape[0]
-    drops = sums.shape[1]
     size = banks[0].shape[0]
-    fields = ((moist, old_moist), (warm, old_warm))
-    outs = (out_moist, out_warm)
-    prepare(fields, (above, below, left, right), padded, side)
+    step_planes = planes // PARTS
+    slots = list(range(arrived.shape[0]))
+    indices = [fetch(start_in, begin, arrived, slots), fetch(back_in, turn, arrived, slots)]
+    copies = []
+    for level, source in enumerate((moist, old_moist, warm, old_warm)):
+        for part in range(PARTS):
+            span = pl.ds(part * step_planes, step_planes)
+            copies.append(fetch(source.at[span], stage.at[level, span], arrived, slots))
+    copies.append(fetch(scaled_in, scaled, arrived, slots))
+    copies.append(fetch(fronts_in, fronts, arrived, slots))
+    copies += [fetch(speed_in.at[k], speed.at[k], arrived, slots) for k in range(3)]
+    fields = ((stage.at[0], stage.at[1]), (stage.at[2], stage.at[3]))
+    outs = (result.at[0], result.at[1])
 
     def clear(step, carry):
         for bank in banks:
@@ -237,23 +359,25 @@
         return carry
 
     lax.fori_loop(0, size // 128, clear, 0)
-    totals = sums[...]
-    drop_vapour = totals[0:1] / totals[2:3]
-    drop_warmth = totals[1:2] / totals[2:3]
-    saturated = 0.5 * jnp.exp(saturation_rate * (drop_warmth - 1.0))
-    for_mass = 2.0 * saturated - drop_vapour
-    for_heat = drop_warmth - 0.5 * for_mass
-    wide = (8, drops)
-    both = jnp.where(
-        (iota(wide, 0) & 1) == 0, jnp.broadcast_to(for_mass, wide), jnp.broadcast_to(for_heat, wide)
-    )
     pieces = []
-    for at in range(0, drops, LANES):
-        piece = both[:, at : min(at + LANES, drops)]
-        if piece.shape[1] < LANES:
-            piece = jnp.concatenate([piece, jnp.zeros((8, LANES - piece.shape[1]), jnp.float32)], axis=1)
-        pieces.append(piece)
-
+    for at in range(0, sums.shape[0], 8):
+        totals = sums[at : at + 8, :]
+        drop_vapour = totals[0:1] / totals[2:3]
+        drop_warmth = totals[1:2] / totals[2:3]
+        saturated = 0.5 * jnp.exp(saturation_rate * (drop_warmth - 1.0))
+        for_mass = 2.0 * saturated - drop_vapour
+        for_heat = drop_warmth - 0.5 * for_mass
+        wide = (8, LANES)
+        pieces.append(
+            jnp.where(
+                (iota(wide, 0) & 1) == 0,
+                jnp.broadcast_to(for_mass, wide),
+                jnp.broadcast_to(for_heat, wide),
+            )
+        )
+    for copy in indices + copies:
+        copy.wait()
+    prepare(fields, (facing, backing, left, right), padded, side)
     lane = iota((8, LANES), 1)
 
     def ready(block):
@@ -272,7 +396,7 @@
     def spill(block, values):
         for half in range(2 * UNROLL):
             for j in range(HALF):
-                at = block * (UNROLL * LANES) + half * HALF + j
+                at = (block * UNROLL + half // 2, half % 2 * HALF + j)
                 entry = jnp.where((lane >> 1) == j, values[half], 0.0)
                 banks[j % len(banks)][pl.ds(begin[at], 8), :] += pltpu.roll(entry, turn[at], 1)
 
@@ -290,6 +414,7 @@
     values = lax.fori_loop(0, count - 1, step, tuple(ready(0)))
     grid_share(count - 1)
     spill(count - 1, values)
+    finished = []
     for plane in range(planes):
         before = (plane - 1) % planes
         for field, out in enumerate(outs):
@@ -298,10 +423,16 @@
                 total = total + bank[pl.ds(plane * rows * 4 + field, rows, stride=4), :]
                 total = total + bank[pl.ds(before * rows * 4 + 2 + field, rows, stride=4), :]
             out[plane] = total
+        if (plane + 1) % step_planes == 0:
+            span = pl.ds(plane + 1 - step_planes, step_planes)
+            for out, target in zip(outs, (out_moist, out_warm)):
+                finished.append(fetch(out.at[span], target.at[span], arrived, slots))
+    for copy in finished:
+        copy.wait()
 
 
 def params(megabytes=40):
-    return pltpu.CompilerParams(vmem_limit_bytes=megabytes << 20)
+    return pltpu.CompilerParams(vmem_limit_bytes=int(megabytes * 1024) << 10)
 
 
 def shards(
@@ -322,90 +453,119 @@
     groups = count // LANES
     f32 = jnp.float32
     shape = jax.ShapeDtypeStruct
-    row_local = lower_base_cell[1, 0] - lax.axis_index("gx") * rows
-    col_local = lower_base_cell[2, 0] - lax.axis_index("gy") * cols
-    turn = (2 * (jnp.arange(count, dtype=jnp.int32) % HALF) - col_local) & 127
-    back = (128 - turn) & 127
-    start = (lower_base_cell[0, 0] * rows + row_local) * 4
+    base = lower_base_cell.reshape(3 * groups, LANES)
     factors = trilinear_factors.reshape(8 * groups, LANES)
     surface = panel_surface.reshape(groups, LANES)
     owner = panel_owner.reshape(groups, LANES)
     field = shape((planes, rows, cols), f32)
 
-    top, bottom, left, right = pl.pallas_call(
-        edges_kernel,
+    head_rows = -(-drops // LANES) * 8
+    edge_rows = 2 * planes * 2
+    spots = shape((groups, LANES), jnp.int32)
+    trays = shape((2 * groups * 8, LANES), f32)
+    start, back, label, scaled, fronts, sums, facing, backing, head, tail = pl.pallas_call(
+        gather_kernel,
         out_shape=(
-            shape((2, planes, 2, cols), f32),
-            shape((2, planes, 2, cols), f32),
+            spots,
+            spots,
+            spots,
+            trays,
+            trays,
+            shape((head_rows, cols), f32),
+            shape((head_rows + edge_rows, cols), f32),
+            shape((edge_rows, cols), f32),
             shape((2, 2 * planes * rows), f32),
             shape((2, 2 * planes * rows), f32),
         ),
-        in_specs=[HBM] * 4,
-        out_specs=[VMEM] * 4,
-        scratch_shapes=[pltpu.VMEM((4, planes, rows, cols), f32), pltpu.SemaphoreType.DMA((8,))],
-        compiler_params=params(EDGES),
-        name="edges",
-    )(gas_moisture, gas_warmth, prior_moisture, prior_warmth)
-
-    def around(axis, head, tail):
+        in_specs=[HBM] * 9,
+        out_specs=[HBM] * 5 + [VMEM] * 5,
+        scratch_shapes=[
+            pltpu.VMEM(base.shape, jnp.int32),
+            pltpu.VMEM((1, 1), jnp.int32),
+            pltpu.VMEM(factors.shape, f32),
+            pltpu.VMEM(surface.shape, f32),
+            pltpu.VMEM(owner.shape, jnp.int32),
+            pltpu.VMEM((planes * rows * 4 + 8, cols), f32),
+            pltpu.VMEM((4, planes, rows, cols), f32),
+            pltpu.VMEM(trays.shape, f32),
+            pltpu.VMEM(trays.shape, f32),
+            pltpu.VMEM((3, groups, LANES), jnp.int32),
+            pltpu.SMEM((groups, LANES), jnp.int32),
+            pltpu.SMEM((groups, LANES), jnp.int32),
+            pltpu.SemaphoreType.DMA((4 * PARTS + 12,)),
+        ],
+        compiler_params=params(GATHER_MB),
+        name="gather",
+    )(
+        base,
+        active_panel_tally,
+        gas_moisture,
+        gas_warmth,
+        prior_moisture,
+        prior_warmth,
+        factors,
+        surface,
+        owner,
+    )
+
+    def permute(x, axis, target):
         size = lax.axis_size(axis)
-        onward = [(i, (i + 1) % size) for i in range(size)]
-        backward = [((i + 1) % size, i) for i in range(size)]
-        return lax.ppermute(tail, axis, onward), lax.ppermute(head, axis, backward)
-
-    above, below = around("gx", top, bottom)
-    from_left, from_right = around("gy", left, right)
-
-    scaled, fronts, sums = pl.pallas_call(
-        gather_kernel,
-        out_shape=(
-            shape((2 * groups * 8, LANES), f32),
-            shape((2 * groups * 8, LANES), f32),
-            shape((8, drops), f32),
-        ),
-        in_specs=[SMEM] * 3 + [VMEM] * 5,
-        out_specs=[VMEM] * 3,
-        scratch_shapes=[pltpu.VMEM((planes * rows * 4 + 8, cols), f32)],
-        compiler_params=params(),
-        name="gather",
-    )(start, turn, active_panel_tally, gas_moisture, gas_warmth, factors, surface, owner)
-
-    totals = sums
+        return lax.ppermute(x, axis, [(i, target(i, size)) for i in range(size)])
+
+    got_facing = permute(facing, "gx", lambda i, n: i ^ 1)
+    got_backing = permute(backing, "gx", lambda i, n: (i - 1 if i % 2 == 0 else i + 1) % n)
+    from_left = permute(tail, "gy", lambda i, n: (i + 1) % n)
+    from_right = permute(head, "gy", lambda i, n: (i - 1) % n)
+    totals = sums + got_facing[0:head_rows]
     size = lax.axis_size("gx")
-    if size & (size - 1):
-        totals = lax.psum(totals, "gx")
-    else:
-        for bit in range(size.bit_length() - 1):
-            swap = [(i, i ^ (1 << bit)) for i in range(size)]
-            totals = totals + lax.ppermute(totals, "gx", swap)
+    stride = 2
+    while stride < size:
+        if size % (2 * stride) == 0:
+            totals = totals + permute(totals, "gx", lambda i, n: i ^ stride)
+            stride *= 2
+        else:
+            partial = totals
+            for number in range(1, size // stride):
+                totals = totals + permute(
+                    partial, "gx", lambda i, n: (i + number * stride) % n
+                )
+            stride = size
 
     size = planes * rows * 4 + 128
     return pl.pallas_call(
         scatter_kernel,
         out_shape=(field, field),
-        in_specs=[SMEM] * 2 + [VMEM] * 13,
-        out_specs=[VMEM] * 2,
+        in_specs=[HBM] * 4 + [VMEM] * 2 + [HBM] * 5 + [VMEM] * 4,
+        out_specs=[HBM] * 2,
         scratch_shapes=[
             pltpu.VMEM((2, planes, rows + 16, cols), f32),
             pltpu.VMEM((2 * planes * rows, cols), f32),
+            pltpu.VMEM((4, planes, rows, cols), f32),
+            pltpu.VMEM((3, planes, rows, cols), jnp.bfloat16),
+            pltpu.VMEM(trays.shape, f32),
+            pltpu.VMEM(trays.shape, f32),
+            pltpu.VMEM((2, planes, rows, cols), f32),
+            pltpu.SMEM((groups, LANES), jnp.int32),
+            pltpu.SMEM((groups, LANES), jnp.int32),
+            pltpu.SemaphoreType.DMA((6 * PARTS + 7,)),
         ]
         + [pltpu.VMEM((size, cols), f32)] * COPIES,
-        compiler_params=params(),
+        compiler_params=params(SCATTER_MB),
         name="scatter",
     )(
         start,
         back,
         scaled,
         fronts,
-        owner,
+        label,
         totals,
         gas_moisture,
         gas_warmth,
         prior_moisture,
         prior_warmth,
         flow_speeds,
-        above,
-        below,
+        got_facing,
+        got_backing,
         from_left,
         from_right,
     )

time: 44.2 us -> 39.6 us (0.90)
  waiting for transfers between devices: 10.9 us -> 4.01 us
  starting transfers between devices: 8.81 us -> 10.8 us
  Pallas kernels: 22.7 us -> 23.3 us
    ppermute x7 -> x6, waiting for transfers between devices: 10.9 us -> 4.01 us  [permute(): return lax.ppermute(x, axis, [(i, target(i, size)) for i in range(size)])]
    ppermute x7 -> x6, starting transfers between devices: 8.81 us -> 10.8 us  [permute(): return lax.ppermute(x, axis, [(i, target(i, size)) for i in range(size)])]
    pallas_call x3 -> x2, Pallas kernels: 22.7 us -> 23.3 us  [the longest x1 12.1 us: shards(): pl.pallas_call(scatter_kernel, out_shape=(field, field), in_specs=[HBM] *...]
  transfers between devices with their start and end apart: 7 -> 6, of which waited for: 3 -> 2; matrix products, arithmetic and copies ran while one was open for 0% -> 0% of each run, Pallas kernels for 20% -> 0%
where the time goes in v4:
time: 39.6 us; the launch traced here: 39.4 us
  Pallas kernels  23.3 us (59%)
  starting transfers between devices  10.8 us (27%)
  waiting for transfers between devices  4.01 us (10%)
  between operations  1.3 us (3%)
    pallas_call x1, Pallas kernels, shards(): pl.pallas_call(scatter_kernel, out_shape=(field, field), in_specs=[HBM] *...  12.1 us
    pallas_call x1, Pallas kernels, shards(): pl.pallas_call(gather_kernel, out_shape=(spots, spots, spots, trays, tray...  11.2 us
    ppermute x6, starting transfers between devices, permute(): return lax.ppermute(x, axis, [(i, target(i, size)) for i in range(size)])  10.8 us
    ppermute x6, waiting for transfers between devices, permute(): return lax.ppermute(x, axis, [(i, target(i, size)) for i in range(size)])  4.01 us
  transfers between devices with their start and end apart: 6, of which 2 were waited for; matrix products, arithmetic and copies ran while one was open for 0% of the time, Pallas kernels for 0%

profile of v4, /device:TPU:0, one launch (start us, length us, event | category | flops | bytes accessed | tf_op | source)
XLA Modules:
  0.0 39.4 jit_solution(13412740464155296855)
XLA Ops:
  1.3 11.2 %gather.1 = (s32[32,128]{1,0:T(8,128)S(1)}, s32[32,128]{1,0:T(8,128)S(1)}, s32[32,128]{1,0:T(8,128)S(1)}, f32[512,128]{1,0:T(8,128)}, f32[512,128]{1,0:T(8,128)}...) custom-call(s32[96,128]{1,0:T(8,128)} %bitcast.5, ...), custom_call_target="tpu_custom_call" | custom-call | tf_op jit(solution)/shard_map/gather/pallas_call | solution.py:466
  12.5 3.0 %collective-permute-start = (f32[80,128]{1,0:T(8,128)}, f32[80,128]{1,0:T(8,128)S(1)}, u32[]{:S(2)}, u32[]{:S(2)}) collective-permute-start(f32[80,128]{1,0:T(8,128)} %get-tuple-element.18), channel_id=1, source_target_pairs={{0,4},{4,0},{8,12},{12,8},{16,20},{20,16},{24,28},{28,24},{1,5},{5... | collective-permute-start | bytes 122888 | tf_op jit(solution)/shard_map/ppermute | solution.py:513
  15.6 3.5 %collective-permute-start.3 = (f32[64,128]{1,0:T(8,128)}, f32[64,128]{1,0:T(8,128)S(1)}, u32[]{:S(2)}, u32[]{:S(2)}) collective-permute-start(f32[64,128]{1,0:T(8,128)} %get-tuple-element.19), channel_id=1, source_target_pairs={{0,28},{4,8},{8,4},{12,16},{16,12},{20,24},{24,20},{28,0},{1,29},{... | collective-permute-start | bytes 98312 | tf_op jit(solution)/shard_map/ppermute | solution.py:513
  19.1 0.0 collective-permute-done.facing
  19.1 0.7 %collective-permute-start.1 = (f32[16,128]{1,0:T(8,128)S(1)}, f32[16,128]{1,0:T(8,128)S(1)}, u32[]{:S(2)}, u32[]{:S(2)}) collective-permute-start(f32[16,128]{1,0:T(8,128)S(1)} %slice_add_fusion), channel_id=1, source_target_pairs={{0,8},{4,12},{8,0},{12,4},{16,24},{20,28},{24,16},{28,20},{1,9},{5... | collective-permute-start | bytes 24584 | tf_op jit(solution)/shard_map/ppermute | solution.py:513
  19.8 0.0 collective-permute-start.4
  19.8 1.7 %collective-permute-start.5 = (f32[2,2048]{1,0:T(2,128)S(1)}, f32[2,2048]{1,0:T(2,128)S(1)}, u32[]{:S(2)}, u32[]{:S(2)}) collective-permute-start(f32[2,2048]{1,0:T(2,128)S(1)} %get-tuple-element.21), channel_id=1, source_target_pairs={{0,3},{1,0},{2,1},{3,2},{4,7},{5,4},{6,5},{7,6},{8,11},{9,8},{10,9... | collective-permute-start | bytes 49160 | tf_op jit(solution)/shard_map/ppermute | solution.py:513
  21.6 1.2 %collective-permute-done.1 = f32[16,128]{1,0:T(8,128)S(1)} collective-permute-done((f32[16,128]{1,0:T(8,128)S(1)}, f32[16,128]{1,0:T(8,128)S(1)}, u32[]{:S(2)}, u32[]{:S(2)}) %collective-permute-start.1) | collective-permute-done | bytes 8224 | tf_op jit(solution)/shard_map/ppermute | solution.py:513
  22.8 1.7 %collective-permute-start.2 = (f32[16,128]{1,0:T(8,128)S(1)}, f32[16,128]{1,0:T(8,128)S(1)}, u32[]{:S(2)}, u32[]{:S(2)}) collective-permute-start(f32[16,128]{1,0:T(8,128)S(1)} %add.10), channel_id=1, source_target_pairs={{0,16},{4,20},{8,24},{12,28},{16,0},{20,4},{24,8},{28,12},{1,17},{... | collective-permute-start | bytes 24584 | tf_op jit(solution)/shard_map/ppermute | solution.py:513
  24.5 2.8 %collective-permute-done.2 = f32[16,128]{1,0:T(8,128)S(1)} collective-permute-done((f32[16,128]{1,0:T(8,128)S(1)}, f32[16,128]{1,0:T(8,128)S(1)}, u32[]{:S(2)}, u32[]{:S(2)}) %collective-permute-start.2) | collective-permute-done | bytes 8224 | tf_op jit(solution)/shard_map/ppermute | solution.py:513
  27.3 0.0 collective-permute-done.4.left
  27.3 0.0 collective-permute-done.5.right
  27.3 0.0 collective-permute-done.3.backing
  27.3 12.1 %scatter.1 = (f32[16,64,128]{2,1,0:T(8,128)}, f32[16,64,128]{2,1,0:T(8,128)}) custom-call(s32[32,128]{1,0:T(8,128)S(1)} %get-tuple-element.12.start_in, s32[32,128]{1,0:T(8,128)S(1)} %get-tuple-element.13.back_in, f32[512,128]{1,0:T(8,128)} %get-tuple-element.14.scaled_in, f32[512,128]{1,0:T(8,128)} %get-tuple-element.15.fronts_in, ...), custom_call_target="tpu_custom_call" | custom-call | tf_op jit(solution)/shard_map/scatter/pallas_call | solution.py:535
  (3 shorter events, 0.0 us)
Async XLA Ops:
  12.5 6.6 %collective-permute-start = (f32[80,128]{1,0:T(8,128)}, f32[80,128]{1,0:T(8,128)S(1)}, u32[]{:S(2)}, u32[]{:S(2)}) collective-permute-start(f32[80,128]{1,0:T(8,128)} %get-tuple-element.18), channel_id=1, source_target_pairs={{0,4},{4,0},{8,12},{12,8},{16,20},{20,16},{24,28},{28,24},{1,5},{5... | collective-permute-start | bytes 122888 | tf_op jit(solution)/shard_map/ppermute | solution.py:513
  15.6 11.8 %collective-permute-start.3 = (f32[64,128]{1,0:T(8,128)}, f32[64,128]{1,0:T(8,128)S(1)}, u32[]{:S(2)}, u32[]{:S(2)}) collective-permute-start(f32[64,128]{1,0:T(8,128)} %get-tuple-element.19), channel_id=1, source_target_pairs={{0,28},{4,8},{8,4},{12,16},{16,12},{20,24},{24,20},{28,0},{1,29},{... | collective-permute-start | bytes 98312 | tf_op jit(solution)/shard_map/ppermute | solution.py:513
  19.1 3.7 %collective-permute-start.1 = (f32[16,128]{1,0:T(8,128)S(1)}, f32[16,128]{1,0:T(8,128)S(1)}, u32[]{:S(2)}, u32[]{:S(2)}) collective-permute-start(f32[16,128]{1,0:T(8,128)S(1)} %slice_add_fusion), channel_id=1, source_target_pairs={{0,8},{4,12},{8,0},{12,4},{16,24},{20,28},{24,16},{28,20},{1,9},{5... | collective-permute-start | bytes 24584 | tf_op jit(solution)/shard_map/ppermute | solution.py:513
  19.8 7.5 %collective-permute-start.4 = (f32[2,2048]{1,0:T(2,128)S(1)}, f32[2,2048]{1,0:T(2,128)S(1)}, u32[]{:S(2)}, u32[]{:S(2)}) collective-permute-start(f32[2,2048]{1,0:T(2,128)S(1)} %get-tuple-element.20), channel_id=1, source_target_pairs={{0,1},{1,2},{2,3},{3,0},{4,5},{5,6},{6,7},{7,4},{8,9},{9,10},{10,1... | collective-permute-start | bytes 49160 | tf_op jit(solution)/shard_map/ppermute | solution.py:513
  19.8 7.5 %collective-permute-start.5 = (f32[2,2048]{1,0:T(2,128)S(1)}, f32[2,2048]{1,0:T(2,128)S(1)}, u32[]{:S(2)}, u32[]{:S(2)}) collective-permute-start(f32[2,2048]{1,0:T(2,128)S(1)} %get-tuple-element.21), channel_id=1, source_target_pairs={{0,3},{1,0},{2,1},{3,2},{4,7},{5,4},{6,5},{7,6},{8,11},{9,8},{10,9... | collective-permute-start | bytes 49160 | tf_op jit(solution)/shard_map/ppermute | solution.py:513
  22.8 4.5 %collective-permute-start.2 = (f32[16,128]{1,0:T(8,128)S(1)}, f32[16,128]{1,0:T(8,128)S(1)}, u32[]{:S(2)}, u32[]{:S(2)}) collective-permute-start(f32[16,128]{1,0:T(8,128)S(1)} %add.10), channel_id=1, source_target_pairs={{0,16},{4,20},{8,24},{12,28},{16,0},{20,4},{24,8},{28,12},{1,17},{... | collective-permute-start | bytes 24584 | tf_op jit(solution)/shard_map/ppermute | solution.py:513

commit v5 on v4

--- a/solution.py
+++ b/solution.py
@@ -23,8 +23,8 @@
 SMEM = pl.BlockSpec(memory_space=pltpu.SMEM)
 COPIES = 4
 UNROLL = 4
-GATHER_MB = 53.85
-SCATTER_MB = 53.65
+GATHER_MB = 16
+SCATTER_MB = 20
 PARTS = 4
 
 
@@ -51,8 +51,8 @@
 
 
 def gather_kernel(
+    tally,
     base_in,
-    tally_in,
     moist,
     warm,
     old_moist,
@@ -60,28 +60,27 @@
     factors_in,
     surface_in,
     owner_in,
+    speed_in,
     start_out,
     back_out,
-    owner_out,
-    scaled_out,
-    fronts_out,
+    owner,
+    scaled,
+    fronts,
+    now,
+    padded,
+    speed,
     sums,
     facing,
     backing,
     head,
     tail,
     base,
-    tally,
     factors,
     surface,
-    owner,
     table,
-    stage,
-    scaled,
-    fronts,
-    places,
+    old,
+    columns,
     start,
-    turn,
     arrived,
 ):
     planes, rows, cols = moist.shape
@@ -97,29 +96,31 @@
             for level in levels:
                 span = pl.ds(part * step_planes, step_planes)
                 source = (moist, old_moist, warm, old_warm)[level]
-                copies.append(fetch(source.at[span], stage.at[level, span], arrived, slots))
+                target = (now, old)[level % 2].at[level // 2, span]
+                copies.append(fetch(source.at[span], target, arrived, slots))
     small = [
         fetch(source, target, arrived, slots)
         for source, target in (
             (factors_in, factors),
             (surface_in, surface),
             (owner_in, owner),
-            (tally_in, tally),
         )
     ]
+    later = [fetch(speed_in.at[k], speed.at[k], arrived, slots) for k in range(3)]
     first.wait()
     spot = (groups, LANES)
     column = base[2 * groups : 3 * groups, :] - lax.axis_index("gy") * cols
-    twist = (2 * (iota(spot, 1) & (HALF - 1)) - column) & 127
     row = base[groups : 2 * groups, :] - lax.axis_index("gx") * rows
-    places[0] = (base[0:groups, :] * rows + row) * 4
-    places[1] = twist
-    places[2] = (128 - twist) & 127
-    indices = [fetch(places.at[0], start, arrived, slots), fetch(places.at[1], turn, arrived, slots)]
-    results = [
-        fetch(places.at[0], start_out, arrived, slots),
-        fetch(places.at[2], back_out, arrived, slots),
-    ]
+    lane = iota((8, LANES), 1)
+    for group in range(groups):
+        wide = jnp.broadcast_to(column[group : group + 1], (8, LANES))
+        for half in range(2):
+            columns[(2 * group + half) * 8 : (2 * group + half) * 8 + 8, :] = (
+                pick(wide, (lane >> 1) + half * HALF) + (lane & 1)
+            )
+    back_out[...] = (column - 2 * (iota(spot, 1) & (HALF - 1))) & 127
+    start_out[...] = (base[0:groups, :] * rows + row) * 4
+    indices = [fetch(start_out, start, arrived, slots)]
     facing[0:head_rows, :] = jnp.zeros((head_rows, LANES), jnp.float32)
     sums[...] = jnp.zeros(sums.shape, jnp.float32)
     for plane in range(planes):
@@ -127,13 +128,12 @@
             copies[plane // step_planes * 2].wait()
             copies[plane // step_planes * 2 + 1].wait()
         below = (plane - 1) % planes
-        table[pl.ds(plane * rows * 4, rows, stride=4), :] = stage[0, plane]
-        table[pl.ds(plane * rows * 4 + 1, rows, stride=4), :] = stage[2, plane]
-        table[pl.ds(below * rows * 4 + 2, rows, stride=4), :] = stage[0, plane]
-        table[pl.ds(below * rows * 4 + 3, rows, stride=4), :] = stage[2, plane]
+        table[pl.ds(plane * rows * 4, rows, stride=4), :] = now[0, plane]
+        table[pl.ds(plane * rows * 4 + 1, rows, stride=4), :] = now[1, plane]
+        table[pl.ds(below * rows * 4 + 2, rows, stride=4), :] = now[0, plane]
+        table[pl.ds(below * rows * 4 + 3, rows, stride=4), :] = now[1, plane]
     for copy in copies[2 * PARTS :] + indices + small:
         copy.wait()
-    results.append(fetch(owner, owner_out, arrived, slots))
     odd = odd_row()
     drops = DROP_DEV * lax.axis_size("gx")
 
@@ -145,7 +145,8 @@
                 halves = []
                 for half in range(2):
                     plane = pair * 2 + half
-                    mixed = 1.5 * stage[2 * field, plane] - 0.5 * stage[2 * field + 1, plane]
+                    mixed = 1.5 * now[field, plane] - 0.5 * old[field, plane]
+                    padded[field, plane, 8 : rows + 8, :] = mixed
                     top, bottom = mixed[0:2], mixed[rows - 2 : rows]
                     at = (field * planes + plane) * 2
                     facing[pl.ds(head_rows + at, 2), :] = jnp.where(odd, top, bottom)
@@ -157,7 +158,7 @@
                 tail[:, pl.ds(at, 2 * rows)] = turned[cols - 2 : cols]
 
     lane = iota((8, LANES), 1)
-    live = jnp.broadcast_to(tally[...], (8, LANES))
+    live = tally[0, 0]
     sub = iota((8, LANES), 0)
     even = (sub & 1) == 0
     even_lane = (lane & 1) == 0
@@ -165,10 +166,12 @@
     def raw(block):
         blocks = []
         for half in range(2 * UNROLL):
+            group = block * UNROLL + half // 2
+            column = columns[pl.ds(pl.multiple_of((group * 2 + half % 2) * 8, 8), 8), :]
             found = jnp.zeros((8, LANES), jnp.float32)
             for j in range(HALF):
-                at = (block * UNROLL + half // 2, half % 2 * HALF + j)
-                entry = pltpu.roll(table[pl.ds(start[at], 8), :], turn[at], 1)
+                at = (group, half % 2 * HALF + j)
+                entry = pick(table[pl.ds(start[at], 8), :], column)
                 found = jnp.where(lane >= 2 * j, entry, found)
             blocks.append(found)
         return blocks
@@ -212,52 +215,32 @@
             preferred_element_type=jnp.float32,
         )
 
-    tray = UNROLL * 16
-    outward = [arrived.at[slots.pop()] for number in range(2)]
-
-    def sends(block):
-        span = pl.ds(pl.multiple_of(block * tray, tray), tray)
-        return [
-            pltpu.make_async_copy(scaled.at[span], scaled_out.at[span], outward[0]),
-            pltpu.make_async_copy(fronts.at[span], fronts_out.at[span], outward[1]),
-        ]
-
-    def send(block):
-        for copy in sends(block):
-            copy.start()
-
     def step(block, carry):
         total, *blocks = carry
         later = raw(block)
         edges(block - 1)
-        total = refine(block - 1, blocks, total)
-        send(block - 1)
-        return (total, *later)
+        return (refine(block - 1, blocks, total), *later)
 
     carry = (jnp.zeros((16, drops), jnp.float32), *raw(0))
     total, *blocks = lax.fori_loop(1, count, step, carry)
     edges(count - 1)
     total = refine(count - 1, blocks, total)
-    send(count - 1)
     total = total[0:8] + total[8:16]
     for number, at in enumerate(range(0, drops, LANES)):
         size = min(LANES, drops - at)
         facing[8 * number : 8 * number + 8, 0:size] = total[:, at : at + size]
         sums[8 * number : 8 * number + 8, 0:size] = total[:, at : at + size]
-    for copy in results:
+    for copy in later:
         copy.wait()
-    pltpu.make_async_copy(scaled, scaled_out, outward[0]).wait()
-    pltpu.make_async_copy(fronts, fronts_out, outward[1]).wait()
-
-
-def prepare(fields, halos, padded, side):
+
+
+def prepare(halos, padded, side):
     facing, backing, left, right = halos
-    planes, rows, cols = fields[0][0].shape
+    planes, rows, cols = padded.shape[1], padded.shape[2] - 16, padded.shape[3]
     head_rows = facing.shape[0] - backing.shape[0]
     odd = odd_row()
-    for field, (now, old) in enumerate(fields):
+    for field in range(2):
         for plane in range(planes):
-            padded[field, plane, 8 : rows + 8, :] = 1.5 * now[plane] - 0.5 * old[plane]
             at = (field * planes + plane) * 2
             near = facing[head_rows + at : head_rows + at + 2, :]
             far = backing[at : at + 2, :]
@@ -276,8 +259,8 @@
             side[pl.ds(at, 2 * rows), :] = block.T
 
 
-def advance(plane, fields, speed, padded, side, outs):
-    planes, rows, cols = fields[0][0].shape
+def advance(plane, now, speed, padded, side, outs):
+    planes, rows, cols = now.shape[1:]
     lane = iota((rows, cols), 1)
     fraction = increment_span / 12.0
     speeds = [speed[k, plane].astype(jnp.float32) * fraction for k in range(3)]
@@ -298,7 +281,7 @@
         ]
         near = 0.0
         far = 0.0
-        total = fields[field][0][plane] - (90.0 * diffusivity * fraction) * center
+        total = now[field, plane] - (90.0 * diffusivity * fraction) * center
         for k, (ahead_one, ahead_two, behind_one, behind_two) in enumerate(around):
             near = near + (ahead_one + behind_one)
             far = far + (ahead_two + behind_two)
@@ -307,50 +290,35 @@
 
 
 def scatter_kernel(
-    start_in,
-    back_in,
-    scaled_in,
-    fronts_in,
+    start,
+    back,
     owner,
+    scaled,
+    fronts,
+    now,
+    padded,
+    speed,
     sums,
-    moist,
-    warm,
-    old_moist,
-    old_warm,
-    speed_in,
     facing,
     backing,
     left,
     right,
     out_moist,
     out_warm,
-    padded,
+    padded_out,
     side,
-    stage,
-    speed,
-    scaled,
-    fronts,
     result,
     begin,
     turn,
     arrived,
     *banks,
 ):
-    planes, rows, cols = moist.shape
+    planes, rows, cols = now.shape[1:]
     groups = owner.shape[0]
     size = banks[0].shape[0]
     step_planes = planes // PARTS
     slots = list(range(arrived.shape[0]))
-    indices = [fetch(start_in, begin, arrived, slots), fetch(back_in, turn, arrived, slots)]
-    copies = []
-    for level, source in enumerate((moist, old_moist, warm, old_warm)):
-        for part in range(PARTS):
-            span = pl.ds(part * step_planes, step_planes)
-            copies.append(fetch(source.at[span], stage.at[level, span], arrived, slots))
-    copies.append(fetch(scaled_in, scaled, arrived, slots))
-    copies.append(fetch(fronts_in, fronts, arrived, slots))
-    copies += [fetch(speed_in.at[k], speed.at[k], arrived, slots) for k in range(3)]
-    fields = ((stage.at[0], stage.at[1]), (stage.at[2], stage.at[3]))
+    indices = [fetch(start, begin, arrived, slots), fetch(back, turn, arrived, slots)]
     outs = (result.at[0], result.at[1])
 
     def clear(step, carry):
@@ -375,9 +343,9 @@
                 jnp.broadcast_to(for_heat, wide),
             )
         )
-    for copy in indices + copies:
+    prepare((facing, backing, left, right), padded_out, side)
+    for copy in indices:
         copy.wait()
-    prepare(fields, (facing, backing, left, right), padded, side)
     lane = iota((8, LANES), 1)
 
     def ready(block):
@@ -402,7 +370,7 @@
 
     def grid_share(block):
         for number in range(planes // count):
-            advance(block * (planes // count) + number, fields, speed, padded, side, outs)
+            advance(block * (planes // count) + number, now, speed, padded_out, side, outs)
 
     def step(block, values):
         later = ready(block + 1)
@@ -463,7 +431,21 @@
     edge_rows = 2 * planes * 2
     spots = shape((groups, LANES), jnp.int32)
     trays = shape((2 * groups * 8, LANES), f32)
-    start, back, label, scaled, fronts, sums, facing, backing, head, tail = pl.pallas_call(
+    pair = shape((2, planes, rows, cols), f32)
+    wide = shape((2, planes, rows + 16, cols), f32)
+    edge = shape((2, 2 * planes * rows), f32)
+    inputs = (
+        base,
+        gas_moisture,
+        gas_warmth,
+        prior_moisture,
+        prior_warmth,
+        factors,
+        surface,
+        owner,
+        flow_speeds,
+    )
+    start, back, label, scaled, fronts, now, blend, speed, sums, facing, backing, head, tail = pl.pallas_call(
         gather_kernel,
         out_shape=(
             spots,
@@ -471,42 +453,30 @@
             spots,
             trays,
             trays,
+            pair,
+            wide,
+            shape(flow_speeds.shape, jnp.bfloat16),
             shape((head_rows, cols), f32),
             shape((head_rows + edge_rows, cols), f32),
             shape((edge_rows, cols), f32),
-            shape((2, 2 * planes * rows), f32),
-            shape((2, 2 * planes * rows), f32),
+            edge,
+            edge,
         ),
-        in_specs=[HBM] * 9,
-        out_specs=[HBM] * 5 + [VMEM] * 5,
+        in_specs=[SMEM] + [HBM] * 9,
+        out_specs=[VMEM] * 13,
         scratch_shapes=[
             pltpu.VMEM(base.shape, jnp.int32),
-            pltpu.VMEM((1, 1), jnp.int32),
             pltpu.VMEM(factors.shape, f32),
             pltpu.VMEM(surface.shape, f32),
-            pltpu.VMEM(owner.shape, jnp.int32),
             pltpu.VMEM((planes * rows * 4 + 8, cols), f32),
-            pltpu.VMEM((4, planes, rows, cols), f32),
-            pltpu.VMEM(trays.shape, f32),
-            pltpu.VMEM(trays.shape, f32),
-            pltpu.VMEM((3, groups, LANES), jnp.int32),
-            pltpu.SMEM((groups, LANES), jnp.int32),
-            pltpu.SMEM((groups, LANES), jnp.int32),
-            pltpu.SemaphoreType.DMA((4 * PARTS + 12,)),
+            pltpu.VMEM(pair.shape, f32),
+            pltpu.VMEM(trays.shape, jnp.int32),
+            pltpu.SMEM(spots.shape, jnp.int32),
+            pltpu.SemaphoreType.DMA((4 * PARTS + 9,)),
         ],
         compiler_params=params(GATHER_MB),
         name="gather",
-    )(
-        base,
-        active_panel_tally,
-        gas_moisture,
-        gas_warmth,
-        prior_moisture,
-        prior_warmth,
-        factors,
-        surface,
-        owner,
-    )
+    )(active_panel_tally, *[pltpu.with_memory_space_constraint(x, pltpu.HBM) for x in inputs])
 
     def permute(x, axis, target):
         size = lax.axis_size(axis)
@@ -534,20 +504,16 @@
     size = planes * rows * 4 + 128
     return pl.pallas_call(
         scatter_kernel,
-        out_shape=(field, field),
-        in_specs=[HBM] * 4 + [VMEM] * 2 + [HBM] * 5 + [VMEM] * 4,
-        out_specs=[HBM] * 2,
+        out_shape=(field, field, wide),
+        in_specs=[VMEM] * 13,
+        out_specs=[HBM] * 2 + [VMEM],
+        input_output_aliases={6: 2},
         scratch_shapes=[
-            pltpu.VMEM((2, planes, rows + 16, cols), f32),
             pltpu.VMEM((2 * planes * rows, cols), f32),
-            pltpu.VMEM((4, planes, rows, cols), f32),
-            pltpu.VMEM((3, planes, rows, cols), jnp.bfloat16),
-            pltpu.VMEM(trays.shape, f32),
-            pltpu.VMEM(trays.shape, f32),
-            pltpu.VMEM((2, planes, rows, cols), f32),
-            pltpu.SMEM((groups, LANES), jnp.int32),
-            pltpu.SMEM((groups, LANES), jnp.int32),
-            pltpu.SemaphoreType.DMA((6 * PARTS + 7,)),
+            pltpu.VMEM(pair.shape, f32),
+            pltpu.SMEM(spots.shape, jnp.int32),
+            pltpu.SMEM(spots.shape, jnp.int32),
+            pltpu.SemaphoreType.DMA((2 * PARTS + 2,)),
         ]
         + [pltpu.VMEM((size, cols), f32)] * COPIES,
         compiler_params=params(SCATTER_MB),
@@ -555,20 +521,18 @@
     )(
         start,
         back,
+        label,
         scaled,
         fronts,
-        label,
+        now,
+        blend,
+        speed,
         totals,
-        gas_moisture,
-        gas_warmth,
-        prior_moisture,
-        prior_warmth,
-        flow_speeds,
         got_facing,
         got_backing,
         from_left,
         from_right,
-    )
+    )[:2]
 
 
 def solution(mesh):

time: 39.6 us -> 35.8 us (0.904)
  Pallas kernels: 23.3 us -> 19.5 us
  waiting for transfers between devices: 4.01 us -> 4.46 us
  starting transfers between devices: 10.8 us -> 10.4 us
    pallas_call x1, Pallas kernels: 11.2 us -> 9.14 us  [shards(): pl.pallas_call(gather_kernel, out_shape=(spots, spots, spots, trays, tray...]
    pallas_call x1, Pallas kernels: 12.1 us -> 10.4 us  [shards(): pl.pallas_call(scatter_kernel, out_shape=(field, field, wide), in_specs=[...]
    ppermute x6, waiting for transfers between devices: 4.01 us -> 4.46 us  [permute(): return lax.ppermute(x, axis, [(i, target(i, size)) for i in range(size)])]
    ppermute x6, starting transfers between devices: 10.8 us -> 10.4 us  [permute(): return lax.ppermute(x, axis, [(i, target(i, size)) for i in range(size)])]
where the time goes in v5:
time: 35.8 us; the launch traced here: 35.7 us
  Pallas kernels  19.5 us (54%)
  starting transfers between devices  10.4 us (29%)
  waiting for transfers between devices  4.46 us (12%)
  between operations  1.31 us (4%)
    pallas_call x1, Pallas kernels, shards(): pl.pallas_call(scatter_kernel, out_shape=(field, field, wide), in_specs=[...  10.4 us
    ppermute x6, starting transfers between devices, permute(): return lax.ppermute(x, axis, [(i, target(i, size)) for i in range(size)])  10.4 us
    pallas_call x1, Pallas kernels, shards(): pl.pallas_call(gather_kernel, out_shape=(spots, spots, spots, trays, tray...  9.14 us
    ppermute x6, waiting for transfers between devices, permute(): return lax.ppermute(x, axis, [(i, target(i, size)) for i in range(size)])  4.46 us
  transfers between devices with their start and end apart: 6, of which 2 were waited for; matrix products, arithmetic and copies ran while one was open for 0% of the time, Pallas kernels for 0%

profile of v5, /device:TPU:0, one launch (start us, length us, event | category | flops | bytes accessed | tf_op | source)
XLA Modules:
  0.0 35.7 jit_solution(1291300943566325112)
XLA Ops:
  1.3 9.1 %gather.1 = (s32[32,128]{1,0:T(8,128)S(1)}, s32[32,128]{1,0:T(8,128)S(1)}, s32[32,128]{1,0:T(8,128)S(1)}, f32[512,128]{1,0:T(8,128)S(1)}, f32[512,128]{1,0:T(8,1...) custom-call(s32[1,1]{1,0:T(1,128)S(6)} %copy.14.tally, ...), custom_call_target="tpu_custom_call" | custom-call | tf_op jit(solution)/shard_map/gather/pallas_call | solution.py:448
  10.4 3.0 %collective-permute-start = (f32[80,128]{1,0:T(8,128)S(1)}, f32[80,128]{1,0:T(8,128)S(1)}, u32[]{:S(2)}, u32[]{:S(2)}) collective-permute-start(f32[80,128]{1,0:T(8,128)S(1)} %get-tuple-element.26), channel_id=1, source_target_pairs={{0,4},{4,0},{8,12},{12,8},{16,20},{20,16},{24,28},{28,24},{1,5},{5... | collective-permute-start | bytes 122888 | tf_op jit(solution)/shard_map/ppermute | solution.py:483
  13.5 3.5 %collective-permute-start.3 = (f32[64,128]{1,0:T(8,128)S(1)}, f32[64,128]{1,0:T(8,128)S(1)}, u32[]{:S(2)}, u32[]{:S(2)}) collective-permute-start(f32[64,128]{1,0:T(8,128)S(1)} %get-tuple-element.27), channel_id=1, source_target_pairs={{0,28},{4,8},{8,4},{12,16},{16,12},{20,24},{24,20},{28,0},{1,29},{... | collective-permute-start | bytes 98312 | tf_op jit(solution)/shard_map/ppermute | solution.py:483
  17.0 0.0 collective-permute-done.facing
  17.0 0.5 %collective-permute-start.1 = (f32[16,128]{1,0:T(8,128)S(1)}, f32[16,128]{1,0:T(8,128)S(1)}, u32[]{:S(2)}, u32[]{:S(2)}) collective-permute-start(f32[16,128]{1,0:T(8,128)S(1)} %slice_add_fusion), channel_id=1, source_target_pairs={{0,8},{4,12},{8,0},{12,4},{16,24},{20,28},{24,16},{28,20},{1,9},{5... | collective-permute-start | bytes 24584 | tf_op jit(solution)/shard_map/ppermute | solution.py:483
  17.5 0.0 collective-permute-start.4
  17.5 1.7 %collective-permute-start.5 = (f32[2,2048]{1,0:T(2,128)S(1)}, f32[2,2048]{1,0:T(2,128)S(1)}, u32[]{:S(2)}, u32[]{:S(2)}) collective-permute-start(f32[2,2048]{1,0:T(2,128)S(1)} %get-tuple-element.29), channel_id=1, source_target_pairs={{0,3},{1,0},{2,1},{3,2},{4,7},{5,4},{6,5},{7,6},{8,11},{9,8},{10,9... | collective-permute-start | bytes 49160 | tf_op jit(solution)/shard_map/ppermute | solution.py:483
  19.3 1.4 %collective-permute-done.1 = f32[16,128]{1,0:T(8,128)S(1)} collective-permute-done((f32[16,128]{1,0:T(8,128)S(1)}, f32[16,128]{1,0:T(8,128)S(1)}, u32[]{:S(2)}, u32[]{:S(2)}) %collective-permute-start.1) | collective-permute-done | bytes 8224 | tf_op jit(solution)/shard_map/ppermute | solution.py:483
  20.7 1.5 %collective-permute-start.2 = (f32[16,128]{1,0:T(8,128)S(1)}, f32[16,128]{1,0:T(8,128)S(1)}, u32[]{:S(2)}, u32[]{:S(2)}) collective-permute-start(f32[16,128]{1,0:T(8,128)S(1)} %add.10), channel_id=1, source_target_pairs={{0,16},{4,20},{8,24},{12,28},{16,0},{20,4},{24,8},{28,12},{1,17},{... | collective-permute-start | bytes 24584 | tf_op jit(solution)/shard_map/ppermute | solution.py:483
  22.2 3.1 %collective-permute-done.2 = f32[16,128]{1,0:T(8,128)S(1)} collective-permute-done((f32[16,128]{1,0:T(8,128)S(1)}, f32[16,128]{1,0:T(8,128)S(1)}, u32[]{:S(2)}, u32[]{:S(2)}) %collective-permute-start.2) | collective-permute-done | bytes 8224 | tf_op jit(solution)/shard_map/ppermute | solution.py:483
  25.2 0.0 collective-permute-done.4.left
  25.3 0.0 collective-permute-done.5.right
  25.3 0.0 collective-permute-done.3.backing
  25.3 10.4 %scatter.1 = (f32[16,64,128]{2,1,0:T(8,128)}, f32[16,64,128]{2,1,0:T(8,128)}, f32[2,16,80,128]{3,2,1,0:T(8,128)S(1)}) custom-call(s32[32,128]{1,0:T(8,128)S(1)} %get-tuple-element.17.start, s32[32,128]{1,0:T(8,128)S(1)} %get-tuple-element.18.back, s32[32,128]{1,0:T(8,128)S(1)} %get-tuple-element.19.owner, ...), custom_call_target="tpu_custom_call", output_to_operand_aliasing={{2}: (6, {})} | custom-call | tf_op jit(solution)/shard_map/scatter/pallas_call | solution.py:505
  (3 shorter events, 0.0 us)
Async XLA Ops:
  10.4 6.6 %collective-permute-start = (f32[80,128]{1,0:T(8,128)S(1)}, f32[80,128]{1,0:T(8,128)S(1)}, u32[]{:S(2)}, u32[]{:S(2)}) collective-permute-start(f32[80,128]{1,0:T(8,128)S(1)} %get-tuple-element.26), channel_id=1, source_target_pairs={{0,4},{4,0},{8,12},{12,8},{16,20},{20,16},{24,28},{28,24},{1,5},{5... | collective-permute-start | bytes 122888 | tf_op jit(solution)/shard_map/ppermute | solution.py:483
  13.5 11.8 %collective-permute-start.3 = (f32[64,128]{1,0:T(8,128)S(1)}, f32[64,128]{1,0:T(8,128)S(1)}, u32[]{:S(2)}, u32[]{:S(2)}) collective-permute-start(f32[64,128]{1,0:T(8,128)S(1)} %get-tuple-element.27), channel_id=1, source_target_pairs={{0,28},{4,8},{8,4},{12,16},{16,12},{20,24},{24,20},{28,0},{1,29},{... | collective-permute-start | bytes 98312 | tf_op jit(solution)/shard_map/ppermute | solution.py:483
  17.0 3.7 %collective-permute-start.1 = (f32[16,128]{1,0:T(8,128)S(1)}, f32[16,128]{1,0:T(8,128)S(1)}, u32[]{:S(2)}, u32[]{:S(2)}) collective-permute-start(f32[16,128]{1,0:T(8,128)S(1)} %slice_add_fusion), channel_id=1, source_target_pairs={{0,8},{4,12},{8,0},{12,4},{16,24},{20,28},{24,16},{28,20},{1,9},{5... | collective-permute-start | bytes 24584 | tf_op jit(solution)/shard_map/ppermute | solution.py:483
  17.5 7.7 %collective-permute-start.4 = (f32[2,2048]{1,0:T(2,128)S(1)}, f32[2,2048]{1,0:T(2,128)S(1)}, u32[]{:S(2)}, u32[]{:S(2)}) collective-permute-start(f32[2,2048]{1,0:T(2,128)S(1)} %get-tuple-element.28), channel_id=1, source_target_pairs={{0,1},{1,2},{2,3},{3,0},{4,5},{5,6},{6,7},{7,4},{8,9},{9,10},{10,1... | collective-permute-start | bytes 49160 | tf_op jit(solution)/shard_map/ppermute | solution.py:483
  17.5 7.7 %collective-permute-start.5 = (f32[2,2048]{1,0:T(2,128)S(1)}, f32[2,2048]{1,0:T(2,128)S(1)}, u32[]{:S(2)}, u32[]{:S(2)}) collective-permute-start(f32[2,2048]{1,0:T(2,128)S(1)} %get-tuple-element.29), channel_id=1, source_target_pairs={{0,3},{1,0},{2,1},{3,2},{4,7},{5,4},{6,5},{7,6},{8,11},{9,8},{10,9... | collective-permute-start | bytes 49160 | tf_op jit(solution)/shard_map/ppermute | solution.py:483
  20.7 4.6 %collective-permute-start.2 = (f32[16,128]{1,0:T(8,128)S(1)}, f32[16,128]{1,0:T(8,128)S(1)}, u32[]{:S(2)}, u32[]{:S(2)}) collective-permute-start(f32[16,128]{1,0:T(8,128)S(1)} %add.10), channel_id=1, source_target_pairs={{0,16},{4,20},{8,24},{12,28},{16,0},{20,4},{24,8},{28,12},{1,17},{... | collective-permute-start | bytes 24584 | tf_op jit(solution)/shard_map/ppermute | solution.py:483

commit v6 on v5

--- a/solution.py
+++ b/solution.py
@@ -22,8 +22,8 @@
 HBM = pl.BlockSpec(memory_space=pltpu.HBM)
 SMEM = pl.BlockSpec(memory_space=pltpu.SMEM)
 COPIES = 4
-UNROLL = 4
-GATHER_MB = 16
+UNROLL = 8
+GATHER_MB = 24
 SCATTER_MB = 20
 PARTS = 4
 

time: 35.8 us -> 35.1 us (0.980)
  Pallas kernels: 19.5 us -> 18.8 us
    pallas_call x1, Pallas kernels: 9.14 us -> 8.39 us  [shards(): pl.pallas_call(gather_kernel, out_shape=(spots, spots, spots, trays, tray...]
where the time goes in v6:
time: 35.1 us; the launch traced here: 34.9 us
  Pallas kernels  18.8 us (54%)
  starting transfers between devices  10.4 us (30%)
  waiting for transfers between devices  4.46 us (13%)
  between operations  1.31 us (4%)
    pallas_call x1, Pallas kernels, shards(): pl.pallas_call(scatter_kernel, out_shape=(field, field, wide), in_specs=[...  10.4 us
    ppermute x6, starting transfers between devices, permute(): return lax.ppermute(x, axis, [(i, target(i, size)) for i in range(size)])  10.4 us
    pallas_call x1, Pallas kernels, shards(): pl.pallas_call(gather_kernel, out_shape=(spots, spots, spots, trays, tray...  8.39 us
    ppermute x6, waiting for transfers between devices, permute(): return lax.ppermute(x, axis, [(i, target(i, size)) for i in range(size)])  4.46 us
  transfers between devices with their start and end apart: 6, of which 2 were waited for; matrix products, arithmetic and copies ran while one was open for 0% of the time, Pallas kernels for 0%

profile of v6, /device:TPU:0, one launch (start us, length us, event | category | flops | bytes accessed | tf_op | source)
XLA Modules:
  0.0 34.9 jit_solution(14740182614551760791)
XLA Ops:
  1.3 8.4 %gather.1 = (s32[32,128]{1,0:T(8,128)S(1)}, s32[32,128]{1,0:T(8,128)S(1)}, s32[32,128]{1,0:T(8,128)S(1)}, f32[512,128]{1,0:T(8,128)S(1)}, f32[512,128]{1,0:T(8,1...) custom-call(s32[1,1]{1,0:T(1,128)S(6)} %copy.14.tally, ...), custom_call_target="tpu_custom_call" | custom-call | tf_op jit(solution)/shard_map/gather/pallas_call | solution.py:448
  9.7 3.0 %collective-permute-start = (f32[80,128]{1,0:T(8,128)S(1)}, f32[80,128]{1,0:T(8,128)S(1)}, u32[]{:S(2)}, u32[]{:S(2)}) collective-permute-start(f32[80,128]{1,0:T(8,128)S(1)} %get-tuple-element.26), channel_id=1, source_target_pairs={{0,4},{4,0},{8,12},{12,8},{16,20},{20,16},{24,28},{28,24},{1,5},{5... | collective-permute-start | bytes 122888 | tf_op jit(solution)/shard_map/ppermute | solution.py:483
  12.7 3.5 %collective-permute-start.3 = (f32[64,128]{1,0:T(8,128)S(1)}, f32[64,128]{1,0:T(8,128)S(1)}, u32[]{:S(2)}, u32[]{:S(2)}) collective-permute-start(f32[64,128]{1,0:T(8,128)S(1)} %get-tuple-element.27), channel_id=1, source_target_pairs={{0,28},{4,8},{8,4},{12,16},{16,12},{20,24},{24,20},{28,0},{1,29},{... | collective-permute-start | bytes 98312 | tf_op jit(solution)/shard_map/ppermute | solution.py:483
  16.2 0.0 collective-permute-done.facing
  16.3 0.5 %collective-permute-start.1 = (f32[16,128]{1,0:T(8,128)S(1)}, f32[16,128]{1,0:T(8,128)S(1)}, u32[]{:S(2)}, u32[]{:S(2)}) collective-permute-start(f32[16,128]{1,0:T(8,128)S(1)} %slice_add_fusion), channel_id=1, source_target_pairs={{0,8},{4,12},{8,0},{12,4},{16,24},{20,28},{24,16},{28,20},{1,9},{5... | collective-permute-start | bytes 24584 | tf_op jit(solution)/shard_map/ppermute | solution.py:483
  16.8 0.0 collective-permute-start.4
  16.8 1.7 %collective-permute-start.5 = (f32[2,2048]{1,0:T(2,128)S(1)}, f32[2,2048]{1,0:T(2,128)S(1)}, u32[]{:S(2)}, u32[]{:S(2)}) collective-permute-start(f32[2,2048]{1,0:T(2,128)S(1)} %get-tuple-element.29), channel_id=1, source_target_pairs={{0,3},{1,0},{2,1},{3,2},{4,7},{5,4},{6,5},{7,6},{8,11},{9,8},{10,9... | collective-permute-start | bytes 49160 | tf_op jit(solution)/shard_map/ppermute | solution.py:483
  18.5 1.4 %collective-permute-done.1 = f32[16,128]{1,0:T(8,128)S(1)} collective-permute-done((f32[16,128]{1,0:T(8,128)S(1)}, f32[16,128]{1,0:T(8,128)S(1)}, u32[]{:S(2)}, u32[]{:S(2)}) %collective-permute-start.1) | collective-permute-done | bytes 8224 | tf_op jit(solution)/shard_map/ppermute | solution.py:483
  19.9 1.5 %collective-permute-start.2 = (f32[16,128]{1,0:T(8,128)S(1)}, f32[16,128]{1,0:T(8,128)S(1)}, u32[]{:S(2)}, u32[]{:S(2)}) collective-permute-start(f32[16,128]{1,0:T(8,128)S(1)} %add.10), channel_id=1, source_target_pairs={{0,16},{4,20},{8,24},{12,28},{16,0},{20,4},{24,8},{28,12},{1,17},{... | collective-permute-start | bytes 24584 | tf_op jit(solution)/shard_map/ppermute | solution.py:483
  21.4 3.1 %collective-permute-done.2 = f32[16,128]{1,0:T(8,128)S(1)} collective-permute-done((f32[16,128]{1,0:T(8,128)S(1)}, f32[16,128]{1,0:T(8,128)S(1)}, u32[]{:S(2)}, u32[]{:S(2)}) %collective-permute-start.2) | collective-permute-done | bytes 8224 | tf_op jit(solution)/shard_map/ppermute | solution.py:483
  24.5 0.0 collective-permute-done.4.left
  24.5 0.0 collective-permute-done.5.right
  24.5 0.0 collective-permute-done.3.backing
  24.5 10.4 %scatter.1 = (f32[16,64,128]{2,1,0:T(8,128)}, f32[16,64,128]{2,1,0:T(8,128)}, f32[2,16,80,128]{3,2,1,0:T(8,128)S(1)}) custom-call(s32[32,128]{1,0:T(8,128)S(1)} %get-tuple-element.17.start, s32[32,128]{1,0:T(8,128)S(1)} %get-tuple-element.18.back, s32[32,128]{1,0:T(8,128)S(1)} %get-tuple-element.19.owner, ...), custom_call_target="tpu_custom_call", output_to_operand_aliasing={{2}: (6, {})} | custom-call | tf_op jit(solution)/shard_map/scatter/pallas_call | solution.py:505
  (3 shorter events, 0.0 us)
Async XLA Ops:
  9.7 6.6 %collective-permute-start = (f32[80,128]{1,0:T(8,128)S(1)}, f32[80,128]{1,0:T(8,128)S(1)}, u32[]{:S(2)}, u32[]{:S(2)}) collective-permute-start(f32[80,128]{1,0:T(8,128)S(1)} %get-tuple-element.26), channel_id=1, source_target_pairs={{0,4},{4,0},{8,12},{12,8},{16,20},{20,16},{24,28},{28,24},{1,5},{5... | collective-permute-start | bytes 122888 | tf_op jit(solution)/shard_map/ppermute | solution.py:483
  12.7 11.8 %collective-permute-start.3 = (f32[64,128]{1,0:T(8,128)S(1)}, f32[64,128]{1,0:T(8,128)S(1)}, u32[]{:S(2)}, u32[]{:S(2)}) collective-permute-start(f32[64,128]{1,0:T(8,128)S(1)} %get-tuple-element.27), channel_id=1, source_target_pairs={{0,28},{4,8},{8,4},{12,16},{16,12},{20,24},{24,20},{28,0},{1,29},{... | collective-permute-start | bytes 98312 | tf_op jit(solution)/shard_map/ppermute | solution.py:483
  16.3 3.7 %collective-permute-start.1 = (f32[16,128]{1,0:T(8,128)S(1)}, f32[16,128]{1,0:T(8,128)S(1)}, u32[]{:S(2)}, u32[]{:S(2)}) collective-permute-start(f32[16,128]{1,0:T(8,128)S(1)} %slice_add_fusion), channel_id=1, source_target_pairs={{0,8},{4,12},{8,0},{12,4},{16,24},{20,28},{24,16},{28,20},{1,9},{5... | collective-permute-start | bytes 24584 | tf_op jit(solution)/shard_map/ppermute | solution.py:483
  16.8 7.7 %collective-permute-start.4 = (f32[2,2048]{1,0:T(2,128)S(1)}, f32[2,2048]{1,0:T(2,128)S(1)}, u32[]{:S(2)}, u32[]{:S(2)}) collective-permute-start(f32[2,2048]{1,0:T(2,128)S(1)} %get-tuple-element.28), channel_id=1, source_target_pairs={{0,1},{1,2},{2,3},{3,0},{4,5},{5,6},{6,7},{7,4},{8,9},{9,10},{10,1... | collective-permute-start | bytes 49160 | tf_op jit(solution)/shard_map/ppermute | solution.py:483
  16.8 7.7 %collective-permute-start.5 = (f32[2,2048]{1,0:T(2,128)S(1)}, f32[2,2048]{1,0:T(2,128)S(1)}, u32[]{:S(2)}, u32[]{:S(2)}) collective-permute-start(f32[2,2048]{1,0:T(2,128)S(1)} %get-tuple-element.29), channel_id=1, source_target_pairs={{0,3},{1,0},{2,1},{3,2},{4,7},{5,4},{6,5},{7,6},{8,11},{9,8},{10,9... | collective-permute-start | bytes 49160 | tf_op jit(solution)/shard_map/ppermute | solution.py:483
  19.9 4.6 %collective-permute-start.2 = (f32[16,128]{1,0:T(8,128)S(1)}, f32[16,128]{1,0:T(8,128)S(1)}, u32[]{:S(2)}, u32[]{:S(2)}) collective-permute-start(f32[16,128]{1,0:T(8,128)S(1)} %add.10), channel_id=1, source_target_pairs={{0,16},{4,20},{8,24},{12,28},{16,0},{20,4},{24,8},{28,12},{1,17},{... | collective-permute-start | bytes 24584 | tf_op jit(solution)/shard_map/ppermute | solution.py:483
